TPU v7x, 32 devices: a whole 2x2x4 slice. The times are simulated.
32 devices in a mesh: groups: 2 (over x), inter: 2 (over core), intra: 8 (over z, y).
Axes of the slice: x: 2, y: 2, z: 4, core: 2. Of those that a mesh axis runs over, the one named last changes fastest.
Arguments:
- tokens: bfloat16 [192, 7168], P(('groups', 'inter', 'intra')), parts along dimension 0, may hold values from -6 to 6
- grad_out: bfloat16 [192, 7168], P(('groups', 'inter', 'intra')), parts along dimension 0, may hold values from -6 to 6
- gate_probs: float32 [192, 2], P(('groups', 'inter', 'intra')), parts along dimension 0, may hold values from 0.1 to 1
- routes: int32 [192, 2], P(('groups', 'inter', 'intra')), parts along dimension 0, may hold values from 0 to 3, all different within a row; in each aligned block of 6 rows (0 to 5, 6 to 11, ...) at most 5 rows name the same one
- w_gate: bfloat16 [4, 608, 7168], P('inter', 'intra'), may hold values from -0.0625 to 0.0625
- w_up: bfloat16 [4, 608, 7168], P('inter', 'intra'), may hold values from -0.0625 to 0.0625
- w_down: bfloat16 [4, 608, 7168], P('inter', 'intra'), may hold values from -0.25 to 0.25
Outputs:
- grad_tokens: bfloat16 [192, 7168], P(('groups', 'inter', 'intra')), parts along dimension 0
- grad_gate: bfloat16 [8, 608, 7168], P(('groups', 'inter'), 'intra'), parts along dimension 0
- grad_up: bfloat16 [8, 608, 7168], P(('groups', 'inter'), 'intra'), parts along dimension 0
- grad_down: bfloat16 [8, 608, 7168], P(('groups', 'inter'), 'intra'), parts along dimension 0
There are 2 independent parts, one for each index of `groups`. A program takes and returns all parts, laid end to end along the dimension named above; an argument that names none is the same for every part. Nothing has to cross between parts.
Inputs may be any that keep to these rules, and one draw needn't show every extreme that they name: `routes`: the 2 experts of a token differ. Among the 6 tokens of one device no expert is named more than 5 times, and in every draw some device names some expert exactly 5 times.
All inputs are finite; a program needn't handle non-finite values.
Results may differ from a plain program's by a relative error of at most 0.014.
Values may be sent and summed in bfloat16 or wider, within the bound.
A program may use at most 192 MiB of HBM per device.

v0:
```python
import jax
import jax.numpy as jnp
from jax import lax
from jax.sharding import PartitionSpec as P


def forward_parts(rows_x, rows_dy, gate_w, up_w, down_w):
    width_contract = (((1,), (1,)), ((), ()))
    gate = lax.dot_general(rows_x, gate_w, width_contract, preferred_element_type=jnp.float32)
    up = lax.dot_general(rows_x, up_w, width_contract, preferred_element_type=jnp.float32)
    sigma = jax.nn.sigmoid(gate)
    silu_gate = gate * sigma
    hidden = (silu_gate * up).astype(jnp.bfloat16)
    grad_hidden = lax.dot_general(
        rows_dy, down_w, width_contract, preferred_element_type=jnp.float32
    )
    grad_pre_gate = (grad_hidden * up * sigma * (1.0 + gate * (1.0 - sigma))).astype(jnp.bfloat16)
    grad_pre_up = (grad_hidden * silu_gate).astype(jnp.bfloat16)
    part = jnp.dot(grad_pre_gate, gate_w, preferred_element_type=jnp.float32)
    part = part + jnp.dot(grad_pre_up, up_w, preferred_element_type=jnp.float32)
    rounded = lax.optimization_barrier(part.astype(jnp.bfloat16))
    return (hidden, grad_pre_gate, grad_pre_up, rounded.astype(jnp.float32))


def weight_terms(saved):
    contract_rows = (((0,), (0,)), ((), ()))
    grads_gate = []
    grads_up = []
    grads_down = []
    for rows_x, rows_dy, hidden, grad_pre_gate, grad_pre_up in saved:
        grads_down.append(
            lax.dot_general(
                hidden, rows_dy, contract_rows, preferred_element_type=jnp.float32
            ).astype(jnp.bfloat16)
        )
        grads_gate.append(
            lax.dot_general(
                grad_pre_gate, rows_x, contract_rows, preferred_element_type=jnp.float32
            ).astype(jnp.bfloat16)
        )
        grads_up.append(
            lax.dot_general(
                grad_pre_up, rows_x, contract_rows, preferred_element_type=jnp.float32
            ).astype(jnp.bfloat16)
        )
    return (
        jnp.stack(grads_gate, axis=0),
        jnp.stack(grads_up, axis=0),
        jnp.stack(grads_down, axis=0),
    )


def return_rows(partials, home_shape):
    summed = lax.psum_scatter(
        partials.astype(jnp.bfloat16), "intra", scatter_dimension=0, tiled=True
    )
    returned = lax.all_to_all(
        summed.reshape(home_shape), "inter", split_axis=0, concat_axis=0, tiled=True
    )
    return returned


def local(tokens, grad_out, gate_probs, routes, w_gate, w_up, w_down):
    tok_count, width = tokens.shape
    top_k = routes.shape[1]
    n_outer = lax.axis_size("inter")
    n_inner = lax.axis_size("intra")
    local_count = w_gate.shape[0]
    n_flight = local_count * n_outer
    capacity = top_k * tok_count // n_flight + 2
    slot_total = n_flight * capacity
    pair_count = tok_count * top_k
    picks = routes.reshape(pair_count)
    one_hot = (picks[:, None] == jnp.arange(n_flight, dtype=jnp.int32)[None, :]).astype(jnp.int32)
    before = jnp.cumsum(one_hot, axis=0) - one_hot
    slot_of = picks * capacity + jnp.sum(before * one_hot, axis=1)
    placing = (slot_of[None, :] == jnp.arange(slot_total, dtype=jnp.int32)[:, None]).astype(
        jnp.bfloat16
    )
    place_tok = jnp.sum(placing.reshape(slot_total, tok_count, top_k), axis=2)
    scaled = (gate_probs[:, :, None] * grad_out[:, None, :].astype(jnp.float32)).astype(
        jnp.bfloat16
    )
    scaled = scaled.reshape(pair_count, width)
    send_x = jnp.dot(place_tok, tokens, preferred_element_type=jnp.float32).astype(jnp.bfloat16)
    send_dy = jnp.dot(placing, scaled, preferred_element_type=jnp.float32).astype(jnp.bfloat16)
    home_shape = (n_outer, local_count, capacity, width)
    across_x, across_dy = (
        lax.all_to_all(
            send_x.reshape(home_shape), "inter", split_axis=0, concat_axis=0, tiled=True
        ),
        lax.all_to_all(
            send_dy.reshape(home_shape), "inter", split_axis=0, concat_axis=0, tiled=True
        ),
    )
    recv_x, recv_dy = (
        lax.all_gather(across_x[None], "intra", axis=0, tiled=True),
        lax.all_gather(across_dy[None], "intra", axis=0, tiled=True),
    )
    row_count = n_inner * n_outer * capacity
    saved = []
    partial_list = []
    for local_expert in range(local_count):
        rows_x = recv_x[:, :, local_expert].reshape(row_count, width)
        rows_dy = recv_dy[:, :, local_expert].reshape(row_count, width)
        hidden, grad_pre_gate, grad_pre_up, partial_value = forward_parts(
            rows_x, rows_dy, w_gate[local_expert], w_up[local_expert], w_down[local_expert]
        )
        saved.append((rows_x, rows_dy, hidden, grad_pre_gate, grad_pre_up))
        partial_list.append(partial_value.reshape(n_inner, n_outer, capacity, width))
    partials = jnp.stack(partial_list, axis=2)
    grad_gate, grad_up, grad_down = weight_terms(saved)
    returned = return_rows(partials, home_shape)
    back_rows = returned.reshape(slot_total, width)
    grad_tokens = lax.dot_general(
        place_tok, back_rows, (((0,), (0,)), ((), ())), preferred_element_type=jnp.float32
    )
    return (grad_tokens.astype(jnp.bfloat16), grad_gate, grad_up, grad_down)


def solution(mesh):
    placed = (
        P(("groups", "inter", "intra"), None),
        P(("groups", "inter", "intra"), None),
        P(("groups", "inter", "intra"), None),
        P(("groups", "inter", "intra"), None),
        P("inter", "intra", None),
        P("inter", "intra", None),
        P("inter", "intra", None),
    )
    return jax.shard_map(
        local,
        mesh=mesh,
        in_specs=placed,
        out_specs=(
            P(("groups", "inter", "intra"), None),
            P(("groups", "inter"), "intra", None),
            P(("groups", "inter"), "intra", None),
            P(("groups", "inter"), "intra", None),
        ),
        check_vma=False,
    )
```

profile of v0, /device:TPU:0, one launch (start us, length us, event | category | flops | bytes accessed | tf_op | source)
XLA Modules:
  0.0 288.5 jit_solution(11996878361638597623)
XLA Ops:
  7.2 0.8 copy.54
  8.0 0.1 eq.35
  8.1 0.2 reduce_window_sum.11
  8.3 0.1 reduce_sum.24
  8.4 0.1 fusion.22
  8.5 0.6 copy-done.18
  9.1 0.3 convolution_convert_fusion.6
  9.4 0.1 reshape.48
  9.6 0.3 copy.60
  9.9 4.7 %all_to_all.15 = bf16[2,2,5,7168]{3,1,2,0:T(2,128)(2,1)} all-to-all(bf16[2,2,5,7168]{3,1,2,0:T(2,128)(2,1)S(1)} %copy.60), channel_id=1, replica_groups=mesh['groups'=2,'inter'=2,'intra'=8] {'inter'}, dimensions={0} | all-to-all | bytes 573440 | tf_op jit(solution)/shard_map/all_to_all | solution.py:89
  14.7 0.1 mul.78
  14.8 0.2 mul.79
  15.0 0.1 copy.56
  15.1 0.1 mul.76
  15.2 0.3 convolution_convert_fusion.7
  15.5 0.1 reshape.47
  15.7 0.3 copy.57
  16.0 4.7 %all_to_all.16 = bf16[2,2,5,7168]{3,1,2,0:T(2,128)(2,1)} all-to-all(bf16[2,2,5,7168]{3,1,2,0:T(2,128)(2,1)S(1)} %copy.57), channel_id=1, replica_groups=mesh['groups'=2,'inter'=2,'intra'=8] {'inter'}, dimensions={0} | all-to-all | bytes 573440 | tf_op jit(solution)/shard_map/all_to_all | solution.py:92
  20.7 0.2 all-reduce.3.cloned.1.call-start
  21.0 4.3 %fusion.26 = (bf16[1,76,7168]{2,0,1:T(2,128)(2,1)}, bf16[1,76,7168]{2,0,1:T(2,128)(2,1)}) fusion(bf16[2,76,7168]{2,0,1:T(2,128)(2,1)S(1)} %copy-done.2), kind=kLoop, calls=%fused_computation.65 | loop fusion | bytes 4358144 | tf_op jit(solution)/shard_map/slice | solution.py:107
  25.3 0.6 dynamic-slice
  25.9 7.0 %fusion.28 = (bf16[1,76,7168]{2,0,1:T(2,128)(2,1)}, bf16[1,76,7168]{2,0,1:T(2,128)(2,1)}) fusion(bf16[2,76,7168]{2,0,1:T(2,128)(2,1)} %param.11), kind=kLoop, calls=%fused_computation.67 | loop fusion | bytes 4358144 | tf_op jit(solution)/shard_map/slice | solution.py:107
  32.9 4.3 %fusion.27 = (bf16[1,76,7168]{2,0,1:T(2,128)(2,1)}, bf16[1,76,7168]{2,0,1:T(2,128)(2,1)}) fusion(bf16[2,76,7168]{2,0,1:T(2,128)(2,1)S(1)} %copy-done.3), kind=kLoop, calls=%fused_computation.66 | loop fusion | bytes 4358144 | tf_op jit(solution)/shard_map/slice | solution.py:107
  37.2 31.6 %all-gather.7.cloned.1.call-done = bf16[16,2,5,7168]{3,1,2,0:T(2,128)(2,1)} async-done(((bf16[2,2,5,7168]{3,1,2,0:T(2,128)(2,1)}), bf16[16,2,5,7168]{3,1,2,0:T(2,128)(2,1)}) %all-gather.7.cloned.1.call-update) | async-done | bytes 2293776 | tf_op jit(solution)/shard_map/all_gather | solution.py:97
  68.8 13.2 %slice_reduce_fusion.2 = (bf16[8,2,5,7168]{3,2,1,0:T(8,128)(2,1)S(1)}, bf16[8,2,5,7168]{3,2,1,0:T(8,128)(2,1)}) fusion(bf16[8,2,2,5,7168]{4,2,3,1,0:T(2,128)(2,1)} %bitcast.67), kind=kLoop, calls=%fused_computation.22 | loop fusion | bytes 4587520 | tf_op jit(solution)/shard_map/slice | solution.py:104
  82.0 0.6 reshape_squeeze.13
  82.6 2.3 fusion.10
  84.9 0.6 fusion.12
  85.5 35.3 %all-gather.5.cloned.1.call-done = bf16[16,2,5,7168]{3,1,2,0:T(2,128)(2,1)} async-done(((bf16[2,2,5,7168]{3,1,2,0:T(2,128)(2,1)}), bf16[16,2,5,7168]{3,1,2,0:T(2,128)(2,1)}) %all-gather.5.cloned.1.call-update) | async-done | bytes 2293776 | tf_op jit(solution)/shard_map/all_gather | solution.py:98
  120.8 13.2 %slice_reduce_fusion.3 = (bf16[8,2,5,7168]{3,2,1,0:T(8,128)(2,1)S(1)}, bf16[8,2,5,7168]{3,2,1,0:T(8,128)(2,1)}) fusion(bf16[8,2,2,5,7168]{4,2,3,1,0:T(2,128)(2,1)} %bitcast.68), kind=kLoop, calls=%fused_computation.23 | loop fusion | bytes 4587520 | tf_op jit(solution)/shard_map/slice | solution.py:105
  134.0 1.4 reshape_squeeze.12
  135.4 2.5 multiply_convert_fusion.6
  137.9 0.5 fusion.4
  138.4 2.0 reshape_squeeze.15
  140.4 2.9 %fusion.13 = f32[80,76]{1,0:T(8,128)} fusion(bf16[80,7168]{1,0:T(8,128)(2,1)S(1)} %reshape_squeeze.15, bf16[1,76,7168]{2,0,1:T(2,128)(2,1)} %get-tuple-element.25), kind=kOutput, calls=%fused_computation.38 | convolution fusion | flops 87162880 | bytes 2260736 | tf_op jit(solution)/shard_map/dot_general | solution.py:10
  143.4 1.2 fusion.15
  144.5 2.5 reshape_squeeze.14
  147.1 2.5 multiply_convert_fusion.4
  149.5 0.5 fusion.5
  150.0 0.2 pad_maximum_fusion.2
  150.3 3.6 %copy.72 = bf16[2,76,7168]{2,0,1:T(2,128)(2,1)} copy(bf16[2,76,7168]{2,1,0:T(8,128)(2,1)S(1)} %pad_maximum_fusion.2) | data formatting | bytes 4358144
  153.9 0.5 fusion.11
  154.4 1.1 copy-done.5
  155.5 0.6 fusion
  156.1 1.5 stack_reshape.8
  157.6 2.3 fusion.14
  159.8 0.6 fusion.1
  160.4 1.5 stack_reshape.9
  161.9 3.0 %pad_maximum_fusion = bf16[8,2,2,5,7168]{4,3,1,0,2:T(8,128)(2,1)S(1)} fusion(bf16[8,2,1,5,7168]{4,3,1,0,2:T(8,128)(2,1)} %stack_reshape.9, bf16[8,2,1,5,7168]{4,3,1,0,2:T(8,128)(2,1)} %stack_reshape.8), kind=kLoop, calls=%fused_computation.19 | loop fusion | flops 1146880 | bytes 4587520 | tf_op jit(solution)/shard_map/stack | solution.py:111
  164.9 4.0 %copy.69 = bf16[8,2,2,5,7168]{4,2,3,1,0:T(2,128)(2,1)} copy(bf16[8,2,2,5,7168]{4,3,1,0,2:T(8,128)(2,1)S(1)} %pad_maximum_fusion) | data formatting | bytes 4587520 | tf_op jit(solution)/shard_map/stack | solution.py:111
  169.0 0.5 fusion.2
  169.5 0.5 fusion.3
  169.9 0.2 pad_maximum_fusion.1
  170.2 3.6 %copy.71 = bf16[2,76,7168]{2,0,1:T(2,128)(2,1)} copy(bf16[2,76,7168]{2,1,0:T(8,128)(2,1)S(1)} %pad_maximum_fusion.1) | data formatting | bytes 4358144
  173.8 0.5 fusion.6
  174.3 0.7 copy-done.10
  175.1 0.5 fusion.7
  175.6 0.2 pad_maximum_fusion.3
  175.8 3.6 %copy.73 = bf16[2,76,7168]{2,0,1:T(2,128)(2,1)} copy(bf16[2,76,7168]{2,1,0:T(8,128)(2,1)S(1)} %pad_maximum_fusion.3) | data formatting | bytes 4358144
  179.4 95.8 %all-reduce.3.cloned.1.call-done = bf16[8,2,2,5,7168]{4,2,3,1,0:T(2,128)(2,1)} async-done(((bf16[8,2,2,5,7168]{4,2,3,1,0:T(2,128)(2,1)}), bf16[8,2,2,5,7168]{4,2,3,1,0:T(2,128)(2,1)}) %all-reduce.3.cloned.1.call-update) | async-done | bytes 2293776
  275.2 1.8 dynamic-slice_bitcast_fusion
  277.0 3.9 %all_to_all.17 = bf16[2,2,5,7168]{3,1,2,0:T(2,128)(2,1)S(1)} all-to-all(bf16[2,2,5,7168]{3,1,2,0:T(2,128)(2,1)S(1)} %dynamic-slice_bitcast_fusion), channel_id=1, replica_groups=mesh['groups'=2,'inter'=2,'intra'=8] {'inter'}, dimensions={0} | all-to-all | bytes 573440 | tf_op jit(solution)/shard_map/all_to_all | solution.py:57
  281.0 0.1 reshape.50
  281.1 0.8 convolution_convert_fusion.8
  (51 shorter events, 0.4 us)
Async XLA Ops:
  7.2 2.0 copy-start
  7.2 7.5 %copy-start.11 = (bf16[6,7168]{1,0:T(8,128)(2,1)S(1)}, bf16[6,7168]{1,0:T(8,128)(2,1)}, u32[]{:S(2)}) copy-start(bf16[6,7168]{1,0:T(8,128)(2,1)} %param.8) | copy-start | bytes 258052
  7.2 61.6 %all-gather.7.cloned.1.call-start = ((), (), s32[]{:S(2)}) async-start(), calls=%async_computation.4 | async-start | bytes 2580480 | tf_op jit(solution)/shard_map/all_gather | solution.py:97
  8.5 0.6 copy-start.18
  9.4 5.6 %copy-start.20 = (f32[6,2]{0,1:T(2,128)S(1)}, f32[6,2]{0,1:T(2,128)}, u32[]{:S(2)}) copy-start(f32[6,2]{0,1:T(2,128)} %param.9) | copy-start | bytes 148
  14.6 106.2 %all-gather.5.cloned.1.call-start = ((), (), s32[]{:S(2)}) async-start(), calls=%async_computation.3 | async-start | bytes 2580480 | tf_op jit(solution)/shard_map/all_gather | solution.py:98
  14.8 6.2 %copy-start.2 = (bf16[2,76,7168]{2,0,1:T(2,128)(2,1)S(1)}, bf16[2,76,7168]{2,0,1:T(2,128)(2,1)}, u32[]{:S(2)}) copy-start(bf16[2,76,7168]{2,0,1:T(2,128)(2,1)} %param.12) | copy-start | bytes 6537220
  20.7 254.5 %all-reduce.3.cloned.1.call-start = ((), (), s32[]{:S(2)}) async-start(), calls=%async_computation.5 | async-start | bytes 4587520
  20.9 4.3 %copy-start.21 = (u32[32]{0:T(128)S(1)}, u32[32]{0:T(128)}, u32[]{:S(2)}) copy-start(u32[32]{0:T(128)} %constant.22) | copy-start | bytes 388
  25.9 7.0 %copy-start.3 = (bf16[2,76,7168]{2,0,1:T(2,128)(2,1)S(1)}, bf16[2,76,7168]{2,0,1:T(2,128)(2,1)}, u32[]{:S(2)}) copy-start(bf16[2,76,7168]{2,0,1:T(2,128)(2,1)} %param.13) | copy-start | bytes 6537220
  82.5 2.4 copy-start.7
  84.9 50.5 %copy-start.12 = (f32[80,76]{1,0:T(8,128)}, f32[80,76]{1,0:T(8,128)S(1)}, u32[]{:S(2)}) copy-start(f32[80,76]{1,0:T(8,128)S(1)} %fusion.10) | copy-start | bytes 72964
  85.5 49.9 %copy-start.14 = (f32[80,76]{1,0:T(8,128)}, f32[80,76]{1,0:T(8,128)S(1)}, u32[]{:S(2)}) copy-start(f32[80,76]{1,0:T(8,128)S(1)} %fusion.12) | copy-start | bytes 72964
  140.4 2.9 %copy-start.6 = (bf16[1,76,7168]{2,0,1:T(2,128)(2,1)S(1)}, bf16[1,76,7168]{2,0,1:T(2,128)(2,1)}, u32[]{:S(2)}) copy-start(bf16[1,76,7168]{2,0,1:T(2,128)(2,1)} %get-tuple-element.29) | copy-start | bytes 3268612
  150.3 3.6 %copy-start.8 = (bf16[1,76,7168]{2,0,1:T(2,128)(2,1)S(1)}, bf16[1,76,7168]{2,0,1:T(2,128)(2,1)}, u32[]{:S(2)}) copy-start(bf16[1,76,7168]{2,0,1:T(2,128)(2,1)} %get-tuple-element.28) | copy-start | bytes 3268612
  153.9 1.6 copy-start.5
  157.6 2.3 copy-start.4
  170.2 3.6 %copy-start.9 = (bf16[80,7168]{1,0:T(8,128)(2,1)S(1)}, bf16[80,7168]{1,0:T(8,128)(2,1)}, u32[]{:S(2)}) copy-start(bf16[80,7168]{1,0:T(8,128)(2,1)} %reshape_squeeze.12) | copy-start | bytes 3440644
  170.2 3.6 %copy-start.13 = (f32[80,76]{1,0:T(8,128)S(1)}, f32[80,76]{1,0:T(8,128)}, u32[]{:S(2)}) copy-start(f32[80,76]{1,0:T(8,128)} %copy-done.12) | copy-start | bytes 72964
  170.2 3.6 %copy-start.15 = (f32[80,76]{1,0:T(8,128)S(1)}, f32[80,76]{1,0:T(8,128)}, u32[]{:S(2)}) copy-start(f32[80,76]{1,0:T(8,128)} %copy-done.14) | copy-start | bytes 72964
  173.8 1.3 copy-start.10
  173.8 1.3 copy-start.16
  173.8 1.3 copy-start.17
  175.8 106.2 %copy-start.1 = (bf16[6,7168]{1,0:T(8,128)(2,1)S(1)}, bf16[6,7168]{1,0:T(8,128)(2,1)}, u32[]{:S(2)}) copy-start(bf16[6,7168]{1,0:T(8,128)(2,1)} %param.7) | copy-start | bytes 258052
  179.4 101.8 %copy-start.19 = (bf16[20,6]{0,1:T(8,128)(2,1)S(1)}, bf16[20,6]{0,1:T(8,128)(2,1)}, u32[]{:S(2)}) copy-start(bf16[20,6]{0,1:T(8,128)(2,1)} %copy-done.18) | copy-start | bytes 724
Sparse Core Ops, SparseCore 0:
  14.7 53.9 all-gather.6
  70.9 49.8 all-gather.4
  169.1 106.0 all-reduce.2
where the time goes:
time: 289 us
  waiting for transfers between devices  163 us (56%)
  local copies, waits for them, and re-layouts  73.8 us (26%)
  matrix products  20.3 us (7%)
  between operations  14.2 us (5%)
  blocking collectives  13.3 us (5%)
  other arithmetic  3.99 us (1%)
    unnamed x4, waiting for transfers between devices  95.9 us
    all_gather x1, waiting for transfers between devices, local(): lax.all_gather(across_dy[None], 'intra', axis=0, tiled=True)  35.3 us
    all_gather x1, waiting for transfers between devices, local(): lax.all_gather(across_x[None], 'intra', axis=0, tiled=True)  31.6 us
    unnamed x50, local copies, waits for them, and re-layouts  14.8 us
    slice x1, local copies, waits for them, and re-layouts, local(): rows_x = recv_x[:, :, local_expert].reshape(row_count, width)  13.2 us
    slice x1, local copies, waits for them, and re-layouts, local(): rows_dy = recv_dy[:, :, local_expert].reshape(row_count, width)  13.2 us
    another operation x3, local copies, waits for them, and re-layouts, local(): partials = jnp.stack(partial_list, axis=2)  7 us
    slice x1, local copies, waits for them, and re-layouts, local(): w_gate[local_expert]  6.98 us
  transfers between devices with their start and end apart: 3, of which 3 were waited for; matrix products, arithmetic and copies ran while one was open for 15% of the time, Pallas kernels for 0%

commit v1 on v0

v1 whole, which is shorter than its diff:
```python
import jax
import jax.numpy as jnp
from jax import lax
from jax.sharding import PartitionSpec as P

BOTH = ("inter", "intra")


def pair_weights(gate_probs, routes, n_flight):
    named = routes[:, :, None] == jnp.arange(n_flight, dtype=jnp.int32)[None, None, :]
    return jnp.sum(jnp.where(named, gate_probs[:, :, None], 0.0), axis=1)


def local(tokens, grad_out, gate_probs, routes, w_gate, w_up, w_down):
    tok_count, width = tokens.shape
    n_outer = lax.axis_size("inter")
    n_inner = lax.axis_size("intra")
    local_count = w_gate.shape[0]
    n_flight = local_count * n_outer
    total = n_outer * n_inner * tok_count
    weights = pair_weights(gate_probs, routes, n_flight)
    rows = jnp.concatenate([tokens, grad_out], axis=0)
    gathered = lax.all_gather(rows, BOTH, axis=0, tiled=False)
    weights = lax.all_gather(weights, BOTH, axis=0, tiled=True)
    x = gathered[:, :tok_count].reshape(total, width)
    dy = gathered[:, tok_count:].reshape(total, width)
    first = lax.axis_index("inter") * local_count
    mine = lax.dynamic_slice_in_dim(weights, first, local_count, axis=1).T[:, :, None]
    f32 = dict(preferred_element_type=jnp.float32)
    gate = jnp.einsum("td,ehd->eth", x, w_gate, **f32)
    up = jnp.einsum("td,ehd->eth", x, w_up, **f32)
    grad_hidden = mine * jnp.einsum("td,ehd->eth", dy, w_down, **f32)
    sigma = jax.nn.sigmoid(gate)
    silu_gate = gate * sigma
    hidden = (mine * silu_gate * up).astype(jnp.bfloat16)
    pre_gate = (grad_hidden * up * sigma * (1.0 + gate * (1.0 - sigma))).astype(jnp.bfloat16)
    pre_up = (grad_hidden * silu_gate).astype(jnp.bfloat16)
    part = jnp.einsum("eth,ehd->td", pre_gate, w_gate, **f32)
    part = part + jnp.einsum("eth,ehd->td", pre_up, w_up, **f32)
    grad_tokens = lax.psum_scatter(
        part.astype(jnp.bfloat16), BOTH, scatter_dimension=0, tiled=True
    )
    grad_down = jnp.einsum("eth,td->ehd", hidden, dy, **f32).astype(jnp.bfloat16)
    grad_gate = jnp.einsum("eth,td->ehd", pre_gate, x, **f32).astype(jnp.bfloat16)
    grad_up = jnp.einsum("eth,td->ehd", pre_up, x, **f32).astype(jnp.bfloat16)
    return (grad_tokens.astype(jnp.bfloat16), grad_gate, grad_up, grad_down)


def solution(mesh):
    row = P(("groups", "inter", "intra"), None)
    weight = P("inter", "intra", None)
    grad = P(("groups", "inter"), "intra", None)
    return jax.shard_map(
        local,
        mesh=mesh,
        in_specs=(row,) * 4 + (weight,) * 3,
        out_specs=(row, grad, grad, grad),
        check_vma=False,
    )
```

time: 289 us -> 174 us (0.60)
  waiting for transfers between devices: 163 us -> 14.3 us
  blocking collectives: 13.3 us -> 84.2 us
  local copies, waits for them, and re-layouts: 73.8 us -> 32.2 us
  starting transfers between devices: 0.3 us -> 14.6 us
  matrix products: 20.3 us -> 10.2 us
    unnamed x4 -> x5, waiting for transfers between devices: 95.9 us -> 0.03 us
    all_gather x2 -> x1, waiting for transfers between devices: 66.9 us -> 14.3 us  [local(): gathered = lax.all_gather(rows, BOTH, axis=0, tiled=False)]
    unnamed x0 -> x1, blocking collectives: none -> 49.6 us
    slice x5 -> x1, local copies, waits for them, and re-layouts: 42 us -> 4.97 us  [local(): x = gathered[:, :tok_count].reshape(total, width)]
    all_gather x0 -> x1, blocking collectives: none -> 34.6 us  [local(): weights = lax.all_gather(weights, BOTH, axis=0, tiled=True)]
    unnamed x1 -> x4, starting transfers between devices: 0.22 us -> 14.6 us
    another operation x7 -> x0, local copies, waits for them, and re-layouts: 13.5 us -> none  [the longest x3 7 us: local(): partials = jnp.stack(partial_list, axis=2)]
    all_to_all x3 -> x0, blocking collectives: 13.3 us -> none  [the longest x1 4.68 us: local(): lax.all_to_all(send_x.reshape(home_shape), 'inter', split_axis=0, concat_...]
  transfers between devices with their start and end apart: 3 -> 5, of which waited for: 3 -> 1; matrix products, arithmetic and copies ran while one was open for 15% -> 9% of each run, Pallas kernels for 0% -> 0%
where the time goes in v1:
time: 174 us; the launch traced here: 173 us
  blocking collectives  84.2 us (48%)
  local copies, waits for them, and re-layouts  32.2 us (19%)
  between operations  14.9 us (9%)
  starting transfers between devices  14.6 us (8%)
  waiting for transfers between devices  14.3 us (8%)
  matrix products  10.2 us (6%)
  other arithmetic  2.57 us (1%)
    unnamed x1, blocking collectives  49.6 us
    all_gather x1, blocking collectives, local(): weights = lax.all_gather(weights, BOTH, axis=0, tiled=True)  34.6 us
    unnamed x42, local copies, waits for them, and re-layouts  22.4 us
    unnamed x4, starting transfers between devices  14.6 us
    all_gather x1, waiting for transfers between devices, local(): gathered = lax.all_gather(rows, BOTH, axis=0, tiled=False)  14.3 us
    slice x1, local copies, waits for them, and re-layouts, local(): x = gathered[:, :tok_count].reshape(total, width)  4.97 us
  transfers between devices with their start and end apart: 5, of which 1 were waited for; matrix products, arithmetic and copies ran while one was open for 9% of the time, Pallas kernels for 0%

profile of v1, /device:TPU:0, one launch (start us, length us, event | category | flops | bytes accessed | tf_op | source)
XLA Modules:
  0.0 173.1 jit_solution(12266041984452228598)
XLA Ops:
  7.2 0.0 copy-start
  7.2 0.0 all-gather.5.cloned.1.call-start
  7.2 1.9 %maximum_bitcast_fusion = bf16[1,12,7168]{2,1,0:T(8,128)(2,1)} fusion(bf16[6,7168]{1,0:T(8,128)(2,1)} %param.8, bf16[6,7168]{1,0:T(8,128)(2,1)} %param.7), kind=kLoop, calls=%fused_computation.19 | loop fusion | flops 344064 | bytes 344064
  9.1 0.0 all-gather.5.cloned.1.call-update
  9.1 0.7 select_reduce_fusion
  9.8 34.6 %all-gather.1 = f32[16,6,4]{1,2,0:T(4,128)S(1)} all-gather(f32[1,6,4]{1,2,0:T(4,128)S(1)} %bitcast.36), channel_id=1, replica_groups=mesh['groups'=2,'inter'=2,'intra'=8] {'inter','intra'}, dimensions={0}, use_global_device_ids=true | all-gather | bytes 1632 | tf_op jit(solution)/shard_map/all_gather | solution.py:24
  44.4 0.1 reshape.21
  44.5 1.2 dynamic-slice.4
  46.4 0.6 dynamic-slice_bitcast_fusion
  47.0 14.3 %all-gather.5.cloned.1.call-done = bf16[16,12,7168]{2,1,0:T(8,128)(2,1)} async-done(((bf16[1,12,7168]{2,1,0:T(8,128)(2,1)}), bf16[16,12,7168]{2,1,0:T(8,128)(2,1)}) %all-gather.5.cloned.1.call-update) | async-done | bytes 2752528 | tf_op jit(solution)/shard_map/all_gather | solution.py:23
  61.3 5.0 %fusion.27 = (bf16[16,6,7168]{2,1,0:T(8,128)(2,1)}, bf16[16,6,7168]{2,1,0:T(8,128)(2,1)}) fusion(bf16[16,12,7168]{2,1,0:T(8,128)(2,1)} %all-gather.5.cloned.1.call-done), kind=kLoop, calls=%fused_computation.31 | loop fusion | bytes 5505024 | tf_op jit(solution)/shard_map/slice | solution.py:25
  66.3 2.6 %reshape.25 = bf16[96,7168,1]{1,0,2:T(8,128)(2,1)} reshape(bf16[16,6,7168]{2,1,0:T(8,128)(2,1)} %get-tuple-element.21) | data formatting | bytes 2752512 | tf_op jit(solution)/shard_map/reshape | solution.py:26
  68.9 1.7 reshape.26
  70.6 0.0 copy-start.1
  70.6 0.0 copy-start.14
  70.6 0.0 copy-start.16
  70.6 2.5 %fusion.11 = f32[2,96,76]{1,2,0:T(8,128)S(1)} fusion(bf16[96,7168,1]{1,0,2:T(8,128)(2,1)S(1)} %reshape.26, bf16[2,76,7168]{2,0,1:T(2,128)(2,1)} %param.12), kind=kOutput, calls=%fused_computation.15 | convolution fusion | flops 209190912 | bytes 3613696 | tf_op jit(solution)/shard_map/td,ehd->eth/dot_general | solution.py:31
  73.1 0.0 copy-done.1
  73.2 0.0 copy-done.14
  73.2 0.1 copy-done.16
  73.3 0.0 copy-start.11
  73.3 0.8 fusion.20
  74.0 0.0 copy-done
  74.1 0.0 copy-start.3
  74.1 1.4 multiply_convert_fusion.2
  75.5 0.0 copy-done.11
  75.5 0.0 copy-start.7
  75.5 0.2 copy-done.3
  75.7 0.7 convolution_bitcast_fusion
  76.3 0.0 copy-done.5
  76.4 0.0 copy-done.7
  76.4 1.8 %fusion.2 = bf16[96,7168]{1,0:T(8,128)(2,1)} fusion(f32[96,7168]{1,0:T(8,128)S(1)} %convolution_bitcast_fusion, bf16[2,96,76]{1,2,0:T(8,128)(2,1)S(1)} %get-tuple-element.22, bf16[2,76,7168]{2,0,1:T(2,128)(2,1)S(1)} %copy-done), kind=kOutput, calls=%fused_computation.6 | convolution fusion | flops 210567168 | bytes 6337024 | tf_op jit(solution)/shard_map/eth,ehd->td/dot_general | solution.py:38
  78.2 49.6 %fusion = bf16[8,7168]{1,0:T(8,128)(2,1)} fusion(bf16[96,7168]{1,0:T(8,128)(2,1)} %fusion.2), kind=kCustom, calls=%all-reduce-scatter | all-reduce-scatter fusion | flops 917505 | bytes 1491456
  127.9 0.0 copy-start.2
  127.9 0.0 copy-start.12
  127.9 0.0 copy-start.13
  127.9 1.0 slice.10
  128.9 3.0 %collective-permute-start = (bf16[8,7168]{1,0:T(8,128)(2,1)}, bf16[8,7168]{1,0:T(8,128)(2,1)S(1)}, u32[]{:S(2)}, u32[]{:S(2)}) collective-permute-start(bf16[8,7168]{1,0:T(8,128)(2,1)} %fusion), channel_id=1, source_target_pairs={{0,1},{1,2},{2,3},{3,4},{4,5},{5,6},{6,7},{7,8},{8,9},{9,10},{10,1... | collective-permute-start | bytes 344072
  131.9 3.8 %collective-permute-start.1 = (bf16[8,7168]{1,0:T(8,128)(2,1)}, bf16[8,7168]{1,0:T(8,128)(2,1)S(1)}, u32[]{:S(2)}, u32[]{:S(2)}) collective-permute-start(bf16[8,7168]{1,0:T(8,128)(2,1)} %fusion), channel_id=1, source_target_pairs={{0,2},{1,3},{2,4},{3,5},{4,6},{5,7},{6,8},{7,9},{8,10},{9,11},{10,... | collective-permute-start | bytes 344072
  135.8 4.8 %collective-permute-start.2 = (bf16[8,7168]{1,0:T(8,128)(2,1)}, bf16[8,7168]{1,0:T(8,128)(2,1)}, u32[]{:S(2)}, u32[]{:S(2)}) collective-permute-start(bf16[8,7168]{1,0:T(8,128)(2,1)} %fusion), channel_id=1, source_target_pairs={{0,3},{1,4},{2,5},{3,6},{4,7},{5,8},{6,9},{7,10},{8,11},{9,12},{10... | collective-permute-start | bytes 344072
  140.6 1.5 convolution_convert_fusion.2
  142.1 0.0 copy-start.6
  142.1 2.9 %collective-permute-start.3 = (bf16[6,7168]{1,0:T(8,128)(2,1)S(1)}, bf16[6,7168]{1,0:T(8,128)(2,1)S(1)}, u32[]{:S(2)}, u32[]{:S(2)}) collective-permute-start(bf16[6,7168]{1,0:T(8,128)(2,1)S(1)} %slice.10), channel_id=1, source_target_pairs={{0,4},{1,5},{2,6},{3,7},{4,8},{5,9},{6,10},{7,11},{8,12},{9,13},{1... | collective-permute-start | bytes 258056
  145.1 0.0 copy-done.2
  145.1 0.0 copy-done.12
  145.1 0.0 copy-done.13
  145.1 0.0 copy-done.15
  145.1 0.8 convolution_convert_fusion
  145.8 0.0 copy-done.6
  145.9 0.7 convolution_convert_fusion.1
  146.6 3.6 %copy.51 = bf16[2,76,7168]{2,0,1:T(2,128)(2,1)} copy(bf16[2,76,7168]{2,1,0:T(8,128)(2,1)S(1)} %convolution_convert_fusion) | data formatting | bytes 4358144
  150.2 3.6 %copy.49 = bf16[2,76,7168]{2,0,1:T(2,128)(2,1)} copy(bf16[2,76,7168]{2,1,0:T(8,128)(2,1)S(1)} %convolution_convert_fusion.2) | data formatting | bytes 4358144
  153.8 3.6 %copy.50 = bf16[2,76,7168]{2,0,1:T(2,128)(2,1)} copy(bf16[2,76,7168]{2,1,0:T(8,128)(2,1)S(1)} %convolution_convert_fusion.1) | data formatting | bytes 4358144
  157.4 0.0 collective-permute-done.3
  157.4 0.0 collective-permute-done
  157.4 0.0 copy-start.8
  157.4 0.0 collective-permute-done.1
  157.4 0.6 copy-done.10
  158.0 0.0 copy-done.8
  158.1 0.6 copy-done.9
  158.7 0.0 collective-permute-done.2
  158.7 0.0 copy-done.4
  158.7 6.9 %concatenate.4 = bf16[38,7168]{1,0:T(8,128)(2,1)S(1)} concatenate(bf16[6,7168]{1,0:T(8,128)(2,1)} %copy-done.10, bf16[8,7168]{1,0:T(8,128)(2,1)} %collective-permute-done.2, bf16[8,7168]{1,0:T(8,128)(2,1)} %copy-done.9, bf16[8,7168]{1,0:T(8,128)(2,1)} %copy-done.8, bf16[8,7168]{1,0:T(8,128)(2,1)S(1)} %copy-done.4), dimensions={0} | concatenate | bytes 1089536
  165.6 0.7 constant_dynamic-slice_fusion
  (6 shorter events, 0.0 us)
Async XLA Ops:
  7.2 66.9 %copy-start = (bf16[2,76,7168]{2,0,1:T(2,128)(2,1)S(1)}, bf16[2,76,7168]{2,0,1:T(2,128)(2,1)}, u32[]{:S(2)}) copy-start(bf16[2,76,7168]{2,0,1:T(2,128)(2,1)} %param.11) | copy-start | bytes 6537220
  7.2 54.1 %all-gather.5.cloned.1.call-start = ((), (), s32[]{:S(2)}) async-start(), calls=%async_computation | async-start | bytes 3899392 | tf_op jit(solution)/shard_map/all_gather | solution.py:23
  70.6 2.6 %copy-start.1 = (bf16[96,7168,1]{1,0,2:T(8,128)(2,1)S(1)}, bf16[96,7168,1]{1,0,2:T(8,128)(2,1)}, u32[]{:S(2)}) copy-start(bf16[96,7168,1]{1,0,2:T(8,128)(2,1)} %reshape.25) | copy-start | bytes 4128772
  70.6 2.6 %copy-start.14 = (f32[2,96]{1,0:T(2,128)S(1)}, f32[2,96]{1,0:T(2,128)}, u32[]{:S(2)}) copy-start(f32[2,96]{1,0:T(2,128)} %dynamic-slice_bitcast_fusion) | copy-start | bytes 2308
  70.6 2.7 %copy-start.16 = (bf16[2,76,7168]{2,0,1:T(2,128)(2,1)S(1)}, bf16[2,76,7168]{2,0,1:T(2,128)(2,1)}, u32[]{:S(2)}) copy-start(bf16[2,76,7168]{2,0,1:T(2,128)(2,1)} %param.13) | copy-start | bytes 6537220
  73.3 2.2 %copy-start.11 = (f32[2,96,76]{1,2,0:T(8,128)}, f32[2,96,76]{1,2,0:T(8,128)S(1)}, u32[]{:S(2)}) copy-start(f32[2,96,76]{1,2,0:T(8,128)S(1)} %fusion.11) | copy-start | bytes 175108
  74.1 1.6 copy-start.3
  75.5 0.9 copy-start.5
  75.5 0.9 copy-start.7
  127.9 17.2 %copy-start.2 = (bf16[96,7168,1]{1,0,2:T(8,128)(2,1)S(1)}, bf16[96,7168,1]{1,0,2:T(8,128)(2,1)}, u32[]{:S(2)}) copy-start(bf16[96,7168,1]{1,0,2:T(8,128)(2,1)} %reshape.25) | copy-start | bytes 4128772
  127.9 17.2 %copy-start.12 = (f32[2,96,76]{1,2,0:T(8,128)S(1)}, f32[2,96,76]{1,2,0:T(8,128)}, u32[]{:S(2)}) copy-start(f32[2,96,76]{1,2,0:T(8,128)} %copy-done.11) | copy-start | bytes 175108
  127.9 17.2 %copy-start.13 = (f32[2,96,76]{1,2,0:T(8,128)S(1)}, f32[2,96,76]{1,2,0:T(8,128)}, u32[]{:S(2)}) copy-start(f32[2,96,76]{1,2,0:T(8,128)} %get-tuple-element.24) | copy-start | bytes 175108
  127.9 17.2 %copy-start.15 = (f32[2,96]{1,0:T(2,128)S(1)}, f32[2,96]{1,0:T(2,128)}, u32[]{:S(2)}) copy-start(f32[2,96]{1,0:T(2,128)} %dynamic-slice_bitcast_fusion) | copy-start | bytes 2308
  128.9 28.5 %collective-permute-start = (bf16[8,7168]{1,0:T(8,128)(2,1)}, bf16[8,7168]{1,0:T(8,128)(2,1)S(1)}, u32[]{:S(2)}, u32[]{:S(2)}) collective-permute-start(bf16[8,7168]{1,0:T(8,128)(2,1)} %fusion), channel_id=1, source_target_pairs={{0,1},{1,2},{2,3},{3,4},{4,5},{5,6},{6,7},{7,8},{8,9},{9,10},{10,1... | collective-permute-start | bytes 344072
  131.9 25.5 %collective-permute-start.1 = (bf16[8,7168]{1,0:T(8,128)(2,1)}, bf16[8,7168]{1,0:T(8,128)(2,1)S(1)}, u32[]{:S(2)}, u32[]{:S(2)}) collective-permute-start(bf16[8,7168]{1,0:T(8,128)(2,1)} %fusion), channel_id=1, source_target_pairs={{0,2},{1,3},{2,4},{3,5},{4,6},{5,7},{6,8},{7,9},{8,10},{9,11},{10,... | collective-permute-start | bytes 344072
  135.8 22.9 %collective-permute-start.2 = (bf16[8,7168]{1,0:T(8,128)(2,1)}, bf16[8,7168]{1,0:T(8,128)(2,1)}, u32[]{:S(2)}, u32[]{:S(2)}) collective-permute-start(bf16[8,7168]{1,0:T(8,128)(2,1)} %fusion), channel_id=1, source_target_pairs={{0,3},{1,4},{2,5},{3,6},{4,7},{5,8},{6,9},{7,10},{8,11},{9,12},{10... | collective-permute-start | bytes 344072
  142.1 3.7 %copy-start.6 = (bf16[2,96,76]{1,2,0:T(8,128)(2,1)S(1)}, bf16[2,96,76]{1,2,0:T(8,128)(2,1)}, u32[]{:S(2)}) copy-start(bf16[2,96,76]{1,2,0:T(8,128)(2,1)} %copy-done.5) | copy-start | bytes 87556
  142.1 15.3 %collective-permute-start.3 = (bf16[6,7168]{1,0:T(8,128)(2,1)S(1)}, bf16[6,7168]{1,0:T(8,128)(2,1)S(1)}, u32[]{:S(2)}, u32[]{:S(2)}) collective-permute-start(bf16[6,7168]{1,0:T(8,128)(2,1)S(1)} %slice.10), channel_id=1, source_target_pairs={{0,4},{1,5},{2,6},{3,7},{4,8},{5,9},{6,10},{7,11},{8,12},{9,13},{1... | collective-permute-start | bytes 258056
  153.8 4.9 %copy-start.4 = (bf16[8,7168]{1,0:T(8,128)(2,1)S(1)}, bf16[8,7168]{1,0:T(8,128)(2,1)}, u32[]{:S(2)}) copy-start(bf16[8,7168]{1,0:T(8,128)(2,1)} %fusion) | copy-start | bytes 344068
  157.4 0.6 copy-start.10
  157.4 0.7 copy-start.8
  158.1 0.6 copy-start.9
Sparse Core Ops, SparseCore 0:
  10.8 50.4 all-gather.4

commit v2 on v1

v2 whole, which is shorter than its diff:
```python
import functools
import jax
import jax.numpy as jnp
from jax import lax
from jax.experimental import pallas as pl
from jax.experimental.pallas import tpu as pltpu
from jax.sharding import PartitionSpec as P

MESH = pl.DeviceIdType.MESH
SLOT_ROWS = 16
BACK_SPLIT = 8
COLUMN = 1024


def lanes_of(n_inner):
    return 2 if n_inner <= 8 else 1


def greet(peers):
    barrier = pltpu.get_barrier_semaphore()
    count = 0
    for condition, device in peers:
        if condition is None:
            pl.semaphore_signal(barrier, inc=1, device_id=device, device_id_type=MESH)
            count = count + 1
        else:

            @pl.when(condition)
            def _(device=device):
                pl.semaphore_signal(barrier, inc=1, device_id=device, device_id_type=MESH)

            count = count + jnp.where(condition, 1, 0)
    pl.semaphore_wait(barrier, count)


def gather_kernel(n_inner, rows_ref, out_ref, own_sem, up_sem, down_sem, side_sem, core_sem, recv_sem):
    n_y = lanes_of(n_inner)
    n_z = n_inner // n_y
    c = lax.axis_index("inter")
    j = lax.axis_index("intra")
    z, y = j // n_y, j % n_y
    has_up, has_down = z < n_z - 1, z > 0
    up = {"intra": j + n_y}
    down = {"intra": j - n_y}
    side = {"intra": z * n_y + (1 - y)}
    core = {"inter": 1 - c}
    peers = [(None, core), (has_up, up), (has_down, down)]
    if n_y == 2:
        peers.append((None, side))
    greet(peers)

    me = c * n_inner + j
    own = pltpu.make_async_copy(rows_ref, out_ref.at[me], own_sem)
    own.start()

    def copy(slot, sems, device, src=None):
        return pltpu.make_async_remote_copy(
            src_ref=out_ref.at[slot] if src is None else src,
            dst_ref=out_ref.at[slot],
            send_sem=sems.at[slot],
            recv_sem=recv_sem.at[slot],
            device_id=device,
            device_id_type=MESH,
        )

    def arrived(slot):
        copy(slot, core_sem, core).wait_recv()

    sent = []

    def send(condition, slot, sems, device, src=None):
        def go():
            copy(slot, sems, device, src).start()

        if condition is None:
            go()
        else:
            pl.when(condition)(go)
        sent.append((condition, slot, sems, device))

    send(has_up, me, up_sem, up, rows_ref)
    send(has_down, me, down_sem, down, rows_ref)
    if n_y == 2:
        send(None, me, side_sem, side, rows_ref)
    send(None, me, core_sem, core, rows_ref)

    def side_arrivals(k):
        for distance in (k, -k) if k else (0,):
            there = z + distance
            exists = (there >= 0) & (there < n_z) if k else None
            slot = c * n_inner + there * n_y + (1 - y)

            def go(slot=slot):
                arrived(slot)
                copy(slot, core_sem, core).start()

            if exists is None:
                go()
            else:
                pl.when(exists)(go)
            sent.append((exists, slot, core_sem, core))

    for k in range(1, n_z):
        for distance, onward, sems, device in (
            (-k, has_up, up_sem, up),
            (k, has_down, down_sem, down),
        ):
            there = z + distance
            exists = (there >= 0) & (there < n_z)
            slot = c * n_inner + there * n_y + y
            pl.when(exists)(functools.partial(arrived, slot))
            send(exists & onward, slot, sems, device)
            if n_y == 2:
                send(exists, slot, side_sem, side)
            send(exists, slot, core_sem, core)
        if n_y == 2:
            side_arrivals(k - 1)
    if n_y == 2:
        side_arrivals(n_z - 1)

    def last(i, carry):
        arrived((1 - c) * n_inner + i)
        return carry

    lax.fori_loop(0, n_inner, last, 0)
    own.wait()
    for condition, slot, sems, device in sent:
        done = copy(slot, sems, device).wait_send
        if condition is None:
            done()
        else:
            pl.when(condition)(done)


def gather_rows(rows, n_outer, n_inner):
    n = n_outer * n_inner
    return pl.pallas_call(
        functools.partial(gather_kernel, n_inner),
        out_shape=jax.ShapeDtypeStruct((n,) + rows.shape, rows.dtype),
        in_specs=[pl.BlockSpec(memory_space=pl.ANY)],
        out_specs=pl.BlockSpec(memory_space=pl.ANY),
        scratch_shapes=[pltpu.SemaphoreType.DMA(())] + [pltpu.SemaphoreType.DMA((n,))] * 5,
        compiler_params=pltpu.CompilerParams(collective_id=0, has_side_effects=True),
        name="gather_rows",
    )(rows)


def back_kernel(
    n_inner, part_ref, out_ref, core_got, kept, side_out, side_got, far_out, far_got,
    core_sem, core_rsem, side_sem, side_rsem, far_sem, far_rsem,
):
    n_y = lanes_of(n_inner)
    n_z = n_inner // n_y
    c = lax.axis_index("inter")
    j = lax.axis_index("intra")
    z, y = j // n_y, j % n_y
    core = {"inter": 1 - c}
    side = {"intra": z * n_y + (1 - y)}

    def far(k):
        return {"intra": ((z + k) % n_z) * n_y + y}

    peers = [(None, core)] + [(None, far(k)) for k in range(1, n_z)]
    if n_y == 2:
        peers.append((None, side))
    greet(peers)
    order = list(range(1, n_z)) + [0]

    def core_copy(k):
        there = (z + k) % n_z * n_y
        return pltpu.make_async_remote_copy(
            src_ref=part_ref.at[pl.ds((1 - c) * n_inner + there, n_y)],
            dst_ref=core_got.at[pl.ds(there, n_y)],
            send_sem=core_sem.at[k],
            recv_sem=core_rsem.at[k],
            device_id=core,
            device_id_type=MESH,
        )

    def side_copy(k):
        return pltpu.make_async_remote_copy(
            src_ref=side_out.at[k],
            dst_ref=side_got.at[k],
            send_sem=side_sem.at[k],
            recv_sem=side_rsem.at[k],
            device_id=side,
            device_id_type=MESH,
        )

    def far_copy(k):
        return pltpu.make_async_remote_copy(
            src_ref=far_out.at[k],
            dst_ref=far_got.at[k],
            send_sem=far_sem.at[k],
            recv_sem=far_rsem.at[k],
            device_id=far(k),
            device_id_type=MESH,
        )

    f32 = jnp.float32
    for k in order:
        core_copy(k).start()
    for k in order:
        core_copy(k).wait_recv()
        there = (z + k) % n_z * n_y

        def paired(lane):
            mine = part_ref[c * n_inner + there + lane].astype(f32)
            return mine + core_got[there + lane].astype(f32)

        if n_y == 2:
            side_out[k] = paired(1 - y).astype(jnp.bfloat16)
            side_copy(k).start()
        kept[k] = paired(y)
    for k in order:
        if n_y == 2:
            side_copy(k).wait_recv()
            kept[k] = kept[k] + side_got[k].astype(f32)
        if k:
            far_out[k] = kept[k].astype(jnp.bfloat16)
            far_copy(k).start()
    total = kept[0]
    for k in range(1, n_z):
        far_copy(k).wait_recv()
        total = total + far_got[k].astype(f32)
    out_ref[...] = total.astype(jnp.bfloat16)
    for k in order:
        core_copy(k).wait_send()
        if n_y == 2:
            side_copy(k).wait_send()
        if k:
            far_copy(k).wait_send()


def sum_back(part, n_inner):
    block = part.shape[1:]
    n_z = n_inner // lanes_of(n_inner)
    bf16 = jnp.bfloat16
    return pl.pallas_call(
        functools.partial(back_kernel, n_inner),
        out_shape=jax.ShapeDtypeStruct(block, bf16),
        in_specs=[pl.BlockSpec(memory_space=pltpu.VMEM)],
        out_specs=pl.BlockSpec(memory_space=pltpu.VMEM),
        scratch_shapes=[
            pltpu.VMEM((n_inner,) + block, bf16),
            pltpu.VMEM((n_z,) + block, jnp.float32),
        ]
        + [pltpu.VMEM((n_z,) + block, bf16)] * 4
        + [pltpu.SemaphoreType.DMA((n_z,))] * 6,
        compiler_params=pltpu.CompilerParams(
            collective_id=1, has_side_effects=True, vmem_limit_bytes=48 << 20
        ),
        name="sum_back",
    )(part)


def grads_kernel(left_ref, rows_ref, gate_ref, up_ref, down_ref):
    local_count = gate_ref.shape[0]
    rows = rows_ref[...]
    for number, out in enumerate((gate_ref, up_ref, down_ref)):
        for e in range(local_count):
            out[e] = jnp.dot(
                left_ref[number * local_count + e], rows, preferred_element_type=jnp.float32
            ).astype(jnp.bfloat16)


def weight_grads(left, rows, shape):
    local_count, hidden, width = shape
    step = COLUMN if width % COLUMN == 0 else width
    out = pl.BlockSpec((local_count, hidden, step), lambda i: (0, 0, i))
    return pl.pallas_call(
        grads_kernel,
        out_shape=[jax.ShapeDtypeStruct(shape, jnp.bfloat16)] * 3,
        grid=(width // step,),
        in_specs=[
            pl.BlockSpec(left.shape, lambda i: (0, 0, 0)),
            pl.BlockSpec((rows.shape[0], step), lambda i: (0, i)),
        ],
        out_specs=[out] * 3,
        compiler_params=pltpu.CompilerParams(vmem_limit_bytes=40 << 20),
        name="weight_grads",
    )(left, rows)


def three_parts(value):
    high = lax.reduce_precision(value, 8, 7)
    middle = lax.reduce_precision(value - high, 8, 7)
    low = value - high - middle
    return jnp.stack([high, middle, low]).astype(jnp.bfloat16)


def local(tokens, grad_out, gate_probs, routes, w_gate, w_up, w_down):
    tok_count, width = tokens.shape
    n_outer = lax.axis_size("inter")
    n_inner = lax.axis_size("intra")
    n = n_outer * n_inner
    local_count, hidden_count, _ = w_gate.shape
    n_flight = local_count * n_outer
    bf16 = jnp.bfloat16
    f32 = dict(preferred_element_type=jnp.float32)

    named = routes[:, :, None] == jnp.arange(n_flight, dtype=jnp.int32)[None, None, :]
    weights = jnp.sum(jnp.where(named, gate_probs[:, :, None], 0.0), axis=1)
    sent = three_parts(weights).reshape(1, 3 * tok_count * n_flight)
    spare = SLOT_ROWS - 2 * tok_count
    sent = jnp.pad(sent, ((0, spare - 1), (0, width - sent.shape[1])))
    rows = jnp.concatenate([tokens, grad_out, sent], axis=0)
    slots = gather_rows(rows, n_outer, n_inner)

    weights = slots[:, 2 * tok_count, : 3 * tok_count * n_flight].astype(jnp.float32)
    weights = jnp.sum(weights.reshape(n, 3, tok_count, n_flight), axis=1)
    first = lax.axis_index("inter") * local_count
    mine = lax.dynamic_slice_in_dim(weights, first, local_count, axis=2)
    mine = jnp.transpose(mine, (2, 0, 1))[:, :, :, None]
    flat = slots.reshape(n * SLOT_ROWS, width)

    def project(w, begin):
        whole = jnp.einsum("td,ehd->eth", flat, w, **f32)
        whole = whole.reshape(local_count, n, SLOT_ROWS, hidden_count)
        return whole[:, :, begin : begin + tok_count]

    gate = project(w_gate, 0)
    up = project(w_up, 0)
    grad_hidden = mine * project(w_down, tok_count)
    sigma = jax.nn.sigmoid(gate)
    silu_gate = gate * sigma
    hidden = (mine * silu_gate * up).astype(bf16)
    pre_gate = (grad_hidden * up * sigma * (1.0 + gate * (1.0 - sigma))).astype(bf16)
    pre_up = (grad_hidden * silu_gate).astype(bf16)

    compact = (local_count, n * tok_count, hidden_count)
    part = jnp.einsum("eth,ehd->td", pre_gate.reshape(compact), w_gate, **f32)
    part = part + jnp.einsum("eth,ehd->td", pre_up.reshape(compact), w_up, **f32)
    part = part.astype(bf16).reshape(n, tok_count, BACK_SPLIT, width // BACK_SPLIT)
    part = jnp.transpose(part, (0, 2, 1, 3)).reshape(n, BACK_SPLIT * tok_count, -1)
    back = sum_back(part, n_inner).reshape(BACK_SPLIT, tok_count, width // BACK_SPLIT)
    grad_tokens = jnp.transpose(back, (1, 0, 2)).reshape(tok_count, width)

    def spread(value, begin):
        after = SLOT_ROWS - tok_count - begin
        value = jnp.pad(value, ((0, 0), (0, 0), (begin, after), (0, 0)))
        value = value.reshape(local_count, n * SLOT_ROWS, hidden_count)
        return jnp.transpose(value, (0, 2, 1))

    left = jnp.concatenate(
        [spread(pre_gate, 0), spread(pre_up, 0), spread(hidden, tok_count)], axis=0
    )
    grad_gate, grad_up, grad_down = weight_grads(left, flat, w_gate.shape)
    return (grad_tokens, grad_gate, grad_up, grad_down)


def solution(mesh):
    row = P(("groups", "inter", "intra"), None)
    weight = P("inter", "intra", None)
    grad = P(("groups", "inter"), "intra", None)
    return jax.shard_map(
        local,
        mesh=mesh,
        in_specs=(row,) * 4 + (weight,) * 3,
        out_specs=(row, grad, grad, grad),
        check_vma=False,
    )
```

time: 174 us -> 86.1 us (0.49)
  blocking collectives: 84.2 us -> 0 us
  Pallas kernels: 0 us -> 51.8 us
  local copies, waits for them, and re-layouts: 32.2 us -> 16.5 us
  starting transfers between devices: 14.6 us -> 0 us
  waiting for transfers between devices: 14.3 us -> 0 us
  between operations: 14.9 us -> 0.82 us
  matrix products: 10.2 us -> 13.1 us
    pallas_call x0 -> x3, Pallas kernels: none -> 51.8 us  [the longest x1 31.3 us: gather_rows(): pl.pallas_call(functools.partial(gather_kernel, n_inner), out_shape=jax.S...]
    unnamed x1 -> x0, blocking collectives: 49.6 us -> none
    all_gather x1 -> x0, blocking collectives: 34.6 us -> none  [local(): weights = lax.all_gather(weights, BOTH, axis=0, tiled=True)]
    unnamed x4 -> x0, starting transfers between devices: 14.6 us -> none
    all_gather x1 -> x0, waiting for transfers between devices: 14.3 us -> none  [local(): gathered = lax.all_gather(rows, BOTH, axis=0, tiled=False)]
    unnamed x42 -> x10, local copies, waits for them, and re-layouts: 22.4 us -> 13.9 us
    slice x1 -> x0, local copies, waits for them, and re-layouts: 4.97 us -> none  [local(): x = gathered[:, :tok_count].reshape(total, width)]
    dot_general x8 -> x5, matrix products: 10.2 us -> 13.1 us  [the longest x3 11.6 us: project(): whole = jnp.einsum('td,ehd->eth', flat, w, **f32)]
  transfers between devices with their start and end apart: 5 -> 0, of which waited for: 1 -> 0; matrix products, arithmetic and copies ran while one was open for 9% -> 0% of each run, Pallas kernels for 0% -> 0%
where the time goes in v2:
time: 86.1 us; the launch traced here: 85.8 us
  Pallas kernels  51.8 us (60%)
  local copies, waits for them, and re-layouts  16.5 us (19%)
  matrix products  13.1 us (15%)
  other arithmetic  3.56 us (4%)
    pallas_call x1, Pallas kernels, gather_rows(): pl.pallas_call(functools.partial(gather_kernel, n_inner), out_shape=jax.S...  31.3 us
    pallas_call x1, Pallas kernels, sum_back(): pl.pallas_call(functools.partial(back_kernel, n_inner), out_shape=jax.Sha...  14.9 us
    unnamed x10, local copies, waits for them, and re-layouts  13.9 us
    dot_general x3, matrix products, project(): whole = jnp.einsum('td,ehd->eth', flat, w, **f32)  11.6 us
    pallas_call x1, Pallas kernels, weight_grads(): pl.pallas_call(grads_kernel, out_shape=[jax.ShapeDtypeStruct(shape, jnp.b...  5.6 us
    concatenate x1, other arithmetic, local(): rows = jnp.concatenate([tokens, grad_out, sent], axis=0)  1.73 us

profile of v2, /device:TPU:0, one launch (start us, length us, event | category | flops | bytes accessed | tf_op | source)
XLA Modules:
  0.0 85.8 jit_solution(5103526680100589553)
XLA Ops:
  0.6 0.0 copy-start
  0.7 0.9 %select_reduce_fusion = f32[6,4]{0,1:T(4,128)S(1)} fusion(f32[6,2]{0,1:T(2,128)} %param.9, s32[6,2]{0,1:T(2,128)} %param.10), kind=kLoop, calls=%fused_computation.29 | loop fusion | flops 120 | bytes 192 | tf_op jit(solution)/shard_map/reduce_sum | solution.py:303
  1.5 0.1 copy.95
  1.7 0.1 convert_element_type.41
  1.8 1.7 %fusion.20.rows_ref = bf16[16,7168]{1,0:T(8,128)(2,1)} fusion(bf16[1,72]{1,0:T(2,128)(2,1)S(1)} %convert_element_type.41, bf16[6,7168]{1,0:T(8,128)(2,1)} %param.8, bf16[6,7168]{1,0:T(8,128)(2,1)} %param.7), kind=kLoop, calls=%fused_computation.18 | loop fusion | flops 917504 | bytes 401552 | tf_op jit(solution)/shard_map/concatenate | solution.py:307
  3.5 31.3 %gather_rows.1 = bf16[16,16,7168]{2,1,0:T(8,128)(2,1)} custom-call(bf16[16,7168]{1,0:T(8,128)(2,1)} %fusion.20.rows_ref), custom_call_target="tpu_custom_call" | custom-call | tf_op jit(solution)/shard_map/gather_rows/pallas_call | solution.py:137
  34.8 0.8 slice_convert_fusion
  35.5 0.1 copy.96
  35.7 0.1 copy.97
  35.7 4.1 %fusion.13 = f32[2,256,76]{1,2,0:T(8,128)S(1)} fusion(bf16[256,7168,1]{1,0,2:T(8,128)(2,1)} %bitcast.50, bf16[2,76,7168]{2,0,1:T(2,128)(2,1)} %param.11), kind=kOutput, calls=%fused_computation.13 | convolution fusion | flops 557842432 | bytes 6004736 | tf_op jit(solution)/shard_map/td,ehd->eth/dot_general | solution.py:318
  39.8 0.1 copy.103
  40.0 0.0 copy-done
  40.0 3.4 %fusion.10 = f32[2,256,76]{1,2,0:T(8,128)S(1)} fusion(bf16[256,7168,1]{1,0,2:T(8,128)(2,1)} %bitcast.51, bf16[2,76,7168]{2,0,1:T(2,128)(2,1)S(1)} %copy-done), kind=kOutput, calls=%fused_computation.12 | convolution fusion | flops 557842432 | bytes 6004736 | tf_op jit(solution)/shard_map/td,ehd->eth/dot_general | solution.py:318
  43.4 0.1 copy.101
  43.5 4.1 %fusion.16 = f32[2,256,76]{1,2,0:T(8,128)S(1)} fusion(bf16[256,7168,1]{1,0,2:T(8,128)(2,1)} %bitcast.52, bf16[2,76,7168]{2,0,1:T(2,128)(2,1)} %param.13), kind=kOutput, calls=%fused_computation.14 | convolution fusion | flops 557842432 | bytes 6004736 | tf_op jit(solution)/shard_map/td,ehd->eth/dot_general | solution.py:318
  47.6 0.1 copy.99
  47.8 0.1 multiply_convert_fusion
  47.9 0.1 copy.104
  48.0 0.1 copy.107
  48.1 0.1 copy.113
  48.2 0.1 copy.112
  48.4 0.1 copy.114
  48.6 0.0 copy-start.2
  48.6 0.7 convolution_bitcast_fusion
  49.3 0.9 %copy-done.2 = bf16[2,76,7168]{2,0,1:T(2,128)(2,1)S(1)} copy-done((bf16[2,76,7168]{2,0,1:T(2,128)(2,1)S(1)}, bf16[2,76,7168]{2,0,1:T(2,128)(2,1)}, u32[]{:S(2)}) %copy-start.2) | copy-done | bytes 2179096
  50.2 0.8 fusion.1
  51.0 0.2 copy.118
  51.3 0.3 copy.110
  51.5 0.3 copy.111.part_ref
  51.8 14.9 %sum_back.1 = bf16[48,896]{1,0:T(8,128)(2,1)S(1)} custom-call(bf16[16,48,896]{2,1,0:T(8,128)(2,1)S(1)} %copy.111.part_ref), custom_call_target="tpu_custom_call" | custom-call | tf_op jit(solution)/shard_map/sum_back/pallas_call | solution.py:239
  66.7 0.7 reshape.98
  67.4 0.0 copy-start.1
  67.4 2.0 %copy-done.1 = bf16[16,16,7168]{2,1,0:T(8,128)(2,1)S(1)} copy-done((bf16[16,16,7168]{2,1,0:T(8,128)(2,1)S(1)}, bf16[16,16,7168]{2,1,0:T(8,128)(2,1)}, u32[]{:S(2)}) %copy-start.1) | copy-done | bytes 3670040
  69.4 5.6 %weight_grads.1 = (bf16[2,76,7168]{2,1,0:T(8,128)(2,1)S(1)}, bf16[2,76,7168]{2,1,0:T(8,128)(2,1)S(1)}, bf16[2,76,7168]{2,1,0:T(8,128)(2,1)S(1)}) custom-call(bf16[6,76,256]{2,1,0:T(8,128)(2,1)S(1)} %pad_maximum_fusion.left_ref, bf16[256,7168]{1,0:T(8,128)(2,1)S(1)} %bitcast.53), custom_call_target="tpu_custom_call" | custom-call | tf_op jit(solution)/shard_map/weight_grads/pallas_call | solution.py:271
  75.0 3.6 %copy.115 = bf16[2,76,7168]{2,0,1:T(2,128)(2,1)} copy(bf16[2,76,7168]{2,1,0:T(8,128)(2,1)S(1)} %get-tuple-element.27) | data formatting | bytes 4358144
  78.6 3.6 %copy.116 = bf16[2,76,7168]{2,0,1:T(2,128)(2,1)} copy(bf16[2,76,7168]{2,1,0:T(8,128)(2,1)S(1)} %get-tuple-element.28) | data formatting | bytes 4358144
  82.2 3.6 %copy.117 = bf16[2,76,7168]{2,0,1:T(2,128)(2,1)} copy(bf16[2,76,7168]{2,1,0:T(8,128)(2,1)S(1)} %get-tuple-element.29) | data formatting | bytes 4358144
  (8 shorter events, 0.2 us)
Async XLA Ops:
  0.6 39.4 %copy-start = (bf16[2,76,7168]{2,0,1:T(2,128)(2,1)S(1)}, bf16[2,76,7168]{2,0,1:T(2,128)(2,1)}, u32[]{:S(2)}) copy-start(bf16[2,76,7168]{2,0,1:T(2,128)(2,1)} %param.12) | copy-start | bytes 6537220
  48.6 1.6 %copy-start.2 = (bf16[2,76,7168]{2,0,1:T(2,128)(2,1)S(1)}, bf16[2,76,7168]{2,0,1:T(2,128)(2,1)}, u32[]{:S(2)}) copy-start(bf16[2,76,7168]{2,0,1:T(2,128)(2,1)} %param.11) | copy-start | bytes 6537220
  67.4 2.0 %copy-start.1 = (bf16[16,16,7168]{2,1,0:T(8,128)(2,1)S(1)}, bf16[16,16,7168]{2,1,0:T(8,128)(2,1)}, u32[]{:S(2)}) copy-start(bf16[16,16,7168]{2,1,0:T(8,128)(2,1)} %gather_rows.1) | copy-start | bytes 11010052

commit v3 on v2

v3 whole, which is shorter than its diff:
```python
import functools
import jax
import jax.numpy as jnp
from jax import lax
from jax.experimental import pallas as pl
from jax.experimental.pallas import tpu as pltpu
from jax.sharding import PartitionSpec as P

MESH = pl.DeviceIdType.MESH
SLOT_ROWS = 16
BACK_SPLIT = 8
COLUMN = 1024
EXTRA = 128


def lanes_of(n_inner):
    return 2 if n_inner <= 8 else 1


def greet(peers):
    barrier = pltpu.get_barrier_semaphore()
    count = 0
    for condition, device in peers:
        if condition is None:
            pl.semaphore_signal(barrier, inc=1, device_id=device, device_id_type=MESH)
            count = count + 1
        else:

            @pl.when(condition)
            def _(device=device):
                pl.semaphore_signal(barrier, inc=1, device_id=device, device_id_type=MESH)

            count = count + jnp.where(condition, 1, 0)
    pl.semaphore_wait(barrier, count)


def forward_kernel(
    n_inner, rows_ref, gate_hbm, up_hbm, down_hbm, compact_ref, slots_out, left_ref, part_ref,
    slots, raw, flat_w, products,
    own_sem, raw_sem, out_sem, up_sem, down_sem, side_sem, core_sem, recv_sem,
):
    n_y = lanes_of(n_inner)
    n_z = n_inner // n_y
    n, _, _ = slots.shape
    hidden_count, local_count, width = gate_hbm.shape
    joint = hidden_count * local_count
    n_flight = local_count * (n // n_inner)
    tok_count = compact_ref.shape[0] // n
    f32, bf16 = jnp.float32, jnp.bfloat16
    c = lax.axis_index("inter")
    j = lax.axis_index("intra")
    z, y = j // n_y, j % n_y
    has_up, has_down = z < n_z - 1, z > 0
    up = {"intra": j + n_y}
    down = {"intra": j - n_y}
    side = {"intra": z * n_y + (1 - y)}
    core = {"inter": 1 - c}
    me = c * n_inner + j
    own = pltpu.make_async_copy(rows_ref, slots.at[me], own_sem)
    own.start()
    loads = [
        pltpu.make_async_copy(w, raw.at[i], raw_sem.at[i])
        for i, w in enumerate((gate_hbm, up_hbm, down_hbm))
    ]
    for load in loads:
        load.start()
    peers = [(None, core), (has_up, up), (has_down, down)]
    if n_y == 2:
        peers.append((None, side))
    greet(peers)

    def copy(slot, sems, device):
        return pltpu.make_async_remote_copy(
            src_ref=slots.at[slot],
            dst_ref=slots.at[slot],
            send_sem=sems.at[slot],
            recv_sem=recv_sem.at[slot],
            device_id=device,
            device_id_type=MESH,
        )

    def arrived(slot):
        copy(slot, core_sem, core).wait_recv()

    own.wait()
    pl.when(has_up)(copy(me, up_sem, up).start)
    pl.when(has_down)(copy(me, down_sem, down).start)
    if n_y == 2:
        copy(me, side_sem, side).start()
    copy(me, core_sem, core).start()

    step = COLUMN if width % COLUMN == 0 else width
    for i, load in enumerate(loads):
        load.wait()

        def lay(k, carry, i=i):
            cols = pl.ds(pl.multiple_of(k * step, step), step)
            flat_w[i, :, cols] = raw[i, :, :, cols].reshape(joint, step)
            return carry

        lax.fori_loop(0, width // step, lay, 0)

    reach = jnp.minimum(z, n_z - 1 - z)

    def nearest(i):
        k = (i + 1) // 2
        near = jnp.where(i % 2 == 0, z + k, z - k)
        far = jnp.where(z < n_z - 1 - z, i, n_z - 1 - i)
        return jnp.where(i <= 2 * reach, near, far)

    def visit(i, carry):
        @pl.when((i > 0) & (i < n_z))
        def _():
            there = nearest(i)
            slot = c * n_inner + there * n_y + y
            arrived(slot)
            pl.when((there < z) & has_up)(copy(slot, up_sem, up).start)
            pl.when((there > z) & has_down)(copy(slot, down_sem, down).start)
            if n_y == 2:
                copy(slot, side_sem, side).start()
            copy(slot, core_sem, core).start()

        @pl.when(i > 0)
        def _():
            there = nearest(i - 1)
            if n_y == 2:
                slot = c * n_inner + there * n_y + (1 - y)
                arrived(slot)
                copy(slot, core_sem, core).start()
            for lane in range(n_y):
                arrived((1 - c) * n_inner + there * n_y + lane)
            places = [outer * n_inner + there * n_y for outer in range(n // n_inner)]
            rows = jnp.concatenate(
                [
                    slots[pl.ds(place, n_y), :, :width].reshape(n_y * SLOT_ROWS, width)
                    for place in places
                ],
                axis=0,
            )
            for w in range(3):
                product = lax.dot_general(
                    rows, flat_w[w], (((1,), (1,)), ((), ())), preferred_element_type=f32
                ).reshape(len(places), n_y, SLOT_ROWS, joint)
                for at, place in enumerate(places):
                    products[w, pl.ds(place, n_y)] = product[at]

        return carry

    lax.fori_loop(0, n_z + 1, visit, 0)
    save = pltpu.make_async_copy(slots, slots_out, out_sem)
    save.start()

    total = n * SLOT_ROWS
    extra = slots[:, :, width:].reshape(total, slots.shape[2] - width).astype(f32)
    lane = lax.broadcasted_iota(jnp.int32, extra.shape, 1)
    column = lax.broadcasted_iota(jnp.int32, (total, joint), 1)
    weight = jnp.zeros((total, joint), f32)
    for e in range(local_count):
        number = c * local_count + e
        named = (lane == number) | (lane == n_flight + number) | (lane == 2 * n_flight + number)
        one = jnp.sum(jnp.where(named, extra, 0.0), axis=1, keepdims=True)
        weight = jnp.where(column % local_count == e, one, weight)
    gate = products[0].reshape(total, joint)
    raised = products[1].reshape(total, joint)
    grad_hidden = products[2].reshape(total, joint)
    grad_hidden = weight * pltpu.roll(grad_hidden, total - tok_count, 0)
    sigma = jax.nn.sigmoid(gate)
    silu_gate = gate * sigma
    hidden = pltpu.roll(weight * silu_gate * raised, tok_count, 0)
    pre_gate = grad_hidden * raised * sigma * (1.0 + gate * (1.0 - sigma))
    pre_up = grad_hidden * silu_gate
    for i, value in enumerate((pre_gate, pre_up, hidden)):
        left_ref[i] = value.T.astype(bf16)
    compact = compact_ref[...]
    few = [
        jnp.dot(compact, value.astype(bf16), preferred_element_type=f32).astype(bf16)
        for value in (pre_gate, pre_up)
    ]
    for k in range(width // step):
        cols = slice(k * step, (k + 1) * step)
        part = jnp.dot(few[0], flat_w[0, :, cols], preferred_element_type=f32)
        part = part + jnp.dot(few[1], flat_w[1, :, cols], preferred_element_type=f32)
        part_ref[:, cols] = part.astype(bf16)

    def sent(i, carry):
        there = nearest(i)
        slot = c * n_inner + there * n_y + y
        pl.when((there <= z) & has_up)(copy(slot, up_sem, up).wait_send)
        pl.when((there >= z) & has_down)(copy(slot, down_sem, down).wait_send)
        copy(slot, core_sem, core).wait_send()
        if n_y == 2:
            copy(slot, side_sem, side).wait_send()
            slot = c * n_inner + there * n_y + (1 - y)
            copy(slot, core_sem, core).wait_send()
        return carry

    lax.fori_loop(0, n_z, sent, 0)
    save.wait()


def forward(rows, weights, n_outer, n_inner, tok_count):
    n = n_outer * n_inner
    hidden_count, local_count, width = weights[0].shape
    joint = hidden_count * local_count
    total = n * SLOT_ROWS
    bf16 = jnp.bfloat16
    there = jnp.arange(n * tok_count, dtype=jnp.int32)
    there = there // tok_count * SLOT_ROWS + there % tok_count
    compact = (there[:, None] == jnp.arange(total, dtype=jnp.int32)[None, :]).astype(bf16)
    anywhere, vmem = pl.BlockSpec(memory_space=pl.ANY), pl.BlockSpec(memory_space=pltpu.VMEM)
    slots = (n,) + rows.shape
    return pl.pallas_call(
        functools.partial(forward_kernel, n_inner),
        out_shape=[
            jax.ShapeDtypeStruct(slots, bf16),
            jax.ShapeDtypeStruct((3, joint, total), bf16),
            jax.ShapeDtypeStruct((n * tok_count, width), bf16),
        ],
        in_specs=[anywhere] * 4 + [vmem],
        out_specs=[anywhere, vmem, vmem],
        scratch_shapes=[
            pltpu.VMEM(slots, bf16),
            pltpu.VMEM((3,) + weights[0].shape, bf16),
            pltpu.VMEM((3, joint, width), bf16),
            pltpu.VMEM((3, n, SLOT_ROWS, joint), jnp.float32),
            pltpu.SemaphoreType.DMA(()),
            pltpu.SemaphoreType.DMA((3,)),
            pltpu.SemaphoreType.DMA(()),
        ]
        + [pltpu.SemaphoreType.DMA((n,))] * 5,
        compiler_params=pltpu.CompilerParams(
            collective_id=0, has_side_effects=True, vmem_limit_bytes=56 << 20
        ),
        name="forward",
    )(rows, *weights, compact)


def back_kernel(
    n_inner, part_ref, out_ref, core_got, kept, side_out, side_got, far_out, far_got,
    core_sem, core_rsem, side_sem, side_rsem, far_sem, far_rsem,
):
    n_y = lanes_of(n_inner)
    n_z = n_inner // n_y
    c = lax.axis_index("inter")
    j = lax.axis_index("intra")
    z, y = j // n_y, j % n_y
    core = {"inter": 1 - c}
    side = {"intra": z * n_y + (1 - y)}

    def far(k):
        return {"intra": ((z + k) % n_z) * n_y + y}

    peers = [(None, core)] + [(None, far(k)) for k in range(1, n_z)]
    if n_y == 2:
        peers.append((None, side))
    greet(peers)
    order = list(range(1, n_z)) + [0]

    def core_copy(k):
        there = (z + k) % n_z * n_y
        return pltpu.make_async_remote_copy(
            src_ref=part_ref.at[pl.ds((1 - c) * n_inner + there, n_y)],
            dst_ref=core_got.at[pl.ds(there, n_y)],
            send_sem=core_sem.at[k],
            recv_sem=core_rsem.at[k],
            device_id=core,
            device_id_type=MESH,
        )

    def side_copy(k):
        return pltpu.make_async_remote_copy(
            src_ref=side_out.at[k],
            dst_ref=side_got.at[k],
            send_sem=side_sem.at[k],
            recv_sem=side_rsem.at[k],
            device_id=side,
            device_id_type=MESH,
        )

    def far_copy(k):
        return pltpu.make_async_remote_copy(
            src_ref=far_out.at[k],
            dst_ref=far_got.at[k],
            send_sem=far_sem.at[k],
            recv_sem=far_rsem.at[k],
            device_id=far(k),
            device_id_type=MESH,
        )

    f32 = jnp.float32
    for k in order:
        core_copy(k).start()
    for k in order:
        core_copy(k).wait_recv()
        there = (z + k) % n_z * n_y

        def paired(lane):
            mine = part_ref[c * n_inner + there + lane].astype(f32)
            return mine + core_got[there + lane].astype(f32)

        if n_y == 2:
            side_out[k] = paired(1 - y).astype(jnp.bfloat16)
            side_copy(k).start()
        kept[k] = paired(y)
    for k in order:
        if n_y == 2:
            side_copy(k).wait_recv()
            kept[k] = kept[k] + side_got[k].astype(f32)
        if k:
            far_out[k] = kept[k].astype(jnp.bfloat16)
            far_copy(k).start()
    total = kept[0]
    for k in range(1, n_z):
        far_copy(k).wait_recv()
        total = total + far_got[k].astype(f32)
    out_ref[...] = total.astype(jnp.bfloat16)
    for k in order:
        core_copy(k).wait_send()
        if n_y == 2:
            side_copy(k).wait_send()
        if k:
            far_copy(k).wait_send()


def sum_back(part, n_inner):
    block = part.shape[1:]
    n_z = n_inner // lanes_of(n_inner)
    bf16 = jnp.bfloat16
    return pl.pallas_call(
        functools.partial(back_kernel, n_inner),
        out_shape=jax.ShapeDtypeStruct(block, bf16),
        in_specs=[pl.BlockSpec(memory_space=pltpu.VMEM)],
        out_specs=pl.BlockSpec(memory_space=pltpu.VMEM),
        scratch_shapes=[
            pltpu.VMEM((n_inner,) + block, bf16),
            pltpu.VMEM((n_z,) + block, jnp.float32),
        ]
        + [pltpu.VMEM((n_z,) + block, bf16)] * 4
        + [pltpu.SemaphoreType.DMA((n_z,))] * 6,
        compiler_params=pltpu.CompilerParams(
            collective_id=1, has_side_effects=True, vmem_limit_bytes=48 << 20
        ),
        name="sum_back",
    )(part)


def grads_kernel(left_ref, rows_ref, *outs):
    rows = rows_ref[...]
    for number, out in enumerate(outs):
        grad = jnp.dot(left_ref[number], rows, preferred_element_type=jnp.float32)
        out[...] = grad.astype(jnp.bfloat16).reshape(out.shape)


def weight_grads(left, rows, shape):
    hidden, local_count, width = shape
    step = COLUMN if width % COLUMN == 0 else width
    out = pl.BlockSpec((hidden, local_count, step), lambda i: (0, 0, i))
    return pl.pallas_call(
        grads_kernel,
        out_shape=[jax.ShapeDtypeStruct(shape, jnp.bfloat16)] * 3,
        grid=(width // step,),
        in_specs=[
            pl.BlockSpec(left.shape, lambda i: (0, 0, 0)),
            pl.BlockSpec((rows.shape[0], step), lambda i: (0, i)),
        ],
        out_specs=[out] * 3,
        compiler_params=pltpu.CompilerParams(vmem_limit_bytes=40 << 20),
        name="weight_grads",
    )(left, rows)


def three_parts(value):
    high = lax.reduce_precision(value, 8, 7)
    middle = lax.reduce_precision(value - high, 8, 7)
    low = value - high - middle
    return [part.astype(jnp.bfloat16) for part in (high, middle, low)]


def local(tokens, grad_out, gate_probs, routes, w_gate, w_up, w_down):
    tok_count, width = tokens.shape
    n_outer = lax.axis_size("inter")
    n_inner = lax.axis_size("intra")
    n = n_outer * n_inner
    n_flight = w_gate.shape[0] * n_outer

    named = routes[:, :, None] == jnp.arange(n_flight, dtype=jnp.int32)[None, None, :]
    weights = jnp.sum(jnp.where(named, gate_probs[:, :, None], 0.0), axis=1)
    extra = jnp.concatenate(three_parts(weights), axis=1)
    extra = jnp.pad(extra, ((0, SLOT_ROWS - tok_count), (0, EXTRA - extra.shape[1])))
    rows = jnp.concatenate([tokens, grad_out], axis=0)
    rows = jnp.pad(rows, ((0, SLOT_ROWS - 2 * tok_count), (0, 0)))
    rows = jnp.concatenate([rows, extra], axis=1)
    turned = [jnp.transpose(w, (1, 0, 2)) for w in (w_gate, w_up, w_down)]
    slots, left, part = forward(rows, turned, n_outer, n_inner, tok_count)

    part = part.reshape(n, tok_count, BACK_SPLIT, width // BACK_SPLIT)
    part = jnp.transpose(part, (0, 2, 1, 3)).reshape(n, BACK_SPLIT * tok_count, -1)
    back = sum_back(part, n_inner).reshape(BACK_SPLIT, tok_count, width // BACK_SPLIT)
    grad_tokens = jnp.transpose(back, (1, 0, 2)).reshape(tok_count, width)

    flat = slots.reshape(n * SLOT_ROWS, width + EXTRA)
    grads = weight_grads(left, flat, turned[0].shape)
    return (grad_tokens, *(jnp.transpose(grad, (1, 0, 2)) for grad in grads))


def solution(mesh):
    row = P(("groups", "inter", "intra"), None)
    weight = P("inter", "intra", None)
    grad = P(("groups", "inter"), "intra", None)
    return jax.shard_map(
        local,
        mesh=mesh,
        in_specs=(row,) * 4 + (weight,) * 3,
        out_specs=(row, grad, grad, grad),
        check_vma=False,
    )
```

time: 86.1 us -> 72.4 us (0.84)
  matrix products: 13.1 us -> 0 us
  local copies, waits for them, and re-layouts: 16.5 us -> 4.91 us
  Pallas kernels: 51.8 us -> 63.3 us
    dot_general x5 -> x0, matrix products: 13.1 us -> none  [the longest x3 11.6 us: project(): whole = jnp.einsum('td,ehd->eth', flat, w, **f32)]
    pallas_call x1, Pallas kernels: 31.3 us -> 42.5 us  [forward(): pl.pallas_call(functools.partial(forward_kernel, n_inner), out_shape=[jax...]
    unnamed x10 -> x5, local copies, waits for them, and re-layouts: 13.9 us -> 3.63 us
    pallas_call x1, Pallas kernels: 14.9 us -> 15.8 us  [sum_back(): pl.pallas_call(functools.partial(back_kernel, n_inner), out_shape=jax.Sha...]
    concatenate x2 -> x3, other arithmetic: 1.76 us -> 1.83 us  [the longest x1 1.05 us: local(): rows = jnp.concatenate([tokens, grad_out], axis=0)]
where the time goes in v3:
time: 72.4 us; the launch traced here: 72.1 us
  Pallas kernels  63.3 us (87%)
  local copies, waits for them, and re-layouts  4.91 us (7%)
  other arithmetic  3.27 us (5%)
    pallas_call x1, Pallas kernels, forward(): pl.pallas_call(functools.partial(forward_kernel, n_inner), out_shape=[jax...  42.5 us
    pallas_call x1, Pallas kernels, sum_back(): pl.pallas_call(functools.partial(back_kernel, n_inner), out_shape=jax.Sha...  15.8 us
    pallas_call x1, Pallas kernels, weight_grads(): pl.pallas_call(grads_kernel, out_shape=[jax.ShapeDtypeStruct(shape, jnp.b...  4.98 us
    unnamed x5, local copies, waits for them, and re-layouts  3.63 us

profile of v3, /device:TPU:0, one launch (start us, length us, event | category | flops | bytes accessed | tf_op | source)
XLA Modules:
  0.0 72.1 jit_solution(10865646607864921175)
XLA Ops:
  0.6 0.7 select_reduce_fusion
  1.4 0.1 copy.18
  1.5 0.1 fusion.12
  1.5 0.7 fusion.3.compact_ref
  2.2 1.0 %fusion.2 = bf16[16,7168]{1,0:T(8,128)(2,1)S(1)} fusion(bf16[6,7168]{1,0:T(8,128)(2,1)} %param.8, bf16[6,7168]{1,0:T(8,128)(2,1)} %param.7), kind=kLoop, calls=%fused_computation.4 | loop fusion | flops 802816 | bytes 401408 | tf_op jit(solution)/shard_map/concatenate | solution.py:390
  3.3 0.7 pad_maximum_fusion.rows_ref
  4.0 42.5 %forward.1 = (bf16[16,16,7296]{2,1,0:T(8,128)(2,1)}, bf16[3,152,256]{2,1,0:T(8,128)(2,1)}, bf16[96,7168]{1,0:T(8,128)(2,1)}) custom-call(bf16[16,7296]{1,0:T(8,128)(2,1)} %pad_maximum_fusion.rows_ref, bf16[76,2,7168]{2,1,0:T(2,128)(2,1)} %bitcast.19, bf16[76,2,7168]{2,1,0:T(2,128)(2,1)} %bitcast.20, bf16[76,2,7168]{2,1,0:T(2,128)(2,1)} %bitcast.21, ...), custom_call_target="tpu_custom_call" | custom-call | tf_op jit(solution)/shard_map/forward/pallas_call | solution.py:212
  46.5 1.6 %copy.22 = bf16[12,8,8,896]{3,2,1,0:T(8,128)(2,1)S(1)} copy(bf16[12,8,8,896]{3,1,2,0:T(8,128)(2,1)} %bitcast.22) | data formatting | bytes 2752512
  48.1 0.3 copy.20
  48.4 0.0 copy-start.1
  48.4 0.3 copy.21.part_ref
  48.6 15.8 %sum_back.1 = bf16[48,896]{1,0:T(8,128)(2,1)S(1)} custom-call(bf16[16,48,896]{2,1,0:T(8,128)(2,1)S(1)} %copy.21.part_ref), custom_call_target="tpu_custom_call" | custom-call | tf_op jit(solution)/shard_map/sum_back/pallas_call | solution.py:329
  64.4 0.7 reshape.46
  65.1 0.0 copy-done.1
  65.1 0.0 copy-start
  65.1 2.1 %copy-done = bf16[16,16,7296]{2,1,0:T(8,128)(2,1)S(1)} copy-done((bf16[16,16,7296]{2,1,0:T(8,128)(2,1)S(1)}, bf16[16,16,7296]{2,1,0:T(8,128)(2,1)}, u32[]{:S(2)}) %copy-start) | copy-done | bytes 3735576
  67.2 5.0 %weight_grads.1 = (bf16[76,2,7168]{2,1,0:T(2,128)(2,1)}, bf16[76,2,7168]{2,1,0:T(2,128)(2,1)}, bf16[76,2,7168]{2,1,0:T(2,128)(2,1)}) custom-call(bf16[3,152,256]{2,1,0:T(8,128)(2,1)S(1)} %copy-done.1, bf16[256,7296]{1,0:T(8,128)(2,1)S(1)} %bitcast.16), custom_call_target="tpu_custom_call" | custom-call | tf_op jit(solution)/shard_map/weight_grads/pallas_call | solution.py:358
  (2 shorter events, 0.0 us)
Async XLA Ops:
  48.4 16.7 %copy-start.1 = (bf16[3,152,256]{2,1,0:T(8,128)(2,1)S(1)}, bf16[3,152,256]{2,1,0:T(8,128)(2,1)}, u32[]{:S(2)}) copy-start(bf16[3,152,256]{2,1,0:T(8,128)(2,1)} %get-tuple-element.11.left_ref) | copy-start | bytes 700420
  65.1 2.1 %copy-start = (bf16[16,16,7296]{2,1,0:T(8,128)(2,1)S(1)}, bf16[16,16,7296]{2,1,0:T(8,128)(2,1)}, u32[]{:S(2)}) copy-start(bf16[16,16,7296]{2,1,0:T(8,128)(2,1)} %get-tuple-element.12) | copy-start | bytes 11206660

commit v4 on v3

--- a/solution.py
+++ b/solution.py
@@ -1,6 +1,7 @@
 import functools
 import jax
 import jax.numpy as jnp
+import numpy as np
 from jax import lax
 from jax.experimental import pallas as pl
 from jax.experimental.pallas import tpu as pltpu
@@ -11,6 +12,7 @@
 BACK_SPLIT = 8
 COLUMN = 1024
 EXTRA = 128
+SEND_SPLIT = 4
 
 
 def lanes_of(n_inner):
@@ -35,9 +37,8 @@
 
 
 def forward_kernel(
-    n_inner, rows_ref, gate_hbm, up_hbm, down_hbm, compact_ref, slots_out, left_ref, part_ref,
-    slots, raw, flat_w, products,
-    own_sem, raw_sem, out_sem, up_sem, down_sem, side_sem, core_sem, recv_sem,
+    n_inner, tokens_ref, cotangent_ref, extra_ref, gate_hbm, up_hbm, down_hbm,
+    slots_out, left_ref, part_ref, slots, wide, raw, flat_w, products, raw_sem, out_sem, up_sem, down_sem, side_sem, core_sem, recv_sem,
 ):
     n_y = lanes_of(n_inner)
     n_z = n_inner // n_y
@@ -45,7 +46,9 @@
     hidden_count, local_count, width = gate_hbm.shape
     joint = hidden_count * local_count
     n_flight = local_count * (n // n_inner)
-    tok_count = compact_ref.shape[0] // n
+    tok_count = tokens_ref.shape[0]
+    both = 2 * tok_count
+    piece = width // SEND_SPLIT
     f32, bf16 = jnp.float32, jnp.bfloat16
     c = lax.axis_index("inter")
     j = lax.axis_index("intra")
@@ -56,14 +59,18 @@
     side = {"intra": z * n_y + (1 - y)}
     core = {"inter": 1 - c}
     me = c * n_inner + j
-    own = pltpu.make_async_copy(rows_ref, slots.at[me], own_sem)
-    own.start()
     loads = [
         pltpu.make_async_copy(w, raw.at[i], raw_sem.at[i])
         for i, w in enumerate((gate_hbm, up_hbm, down_hbm))
     ]
     for load in loads:
         load.start()
+    slots[me, :, piece:] = jnp.zeros((SEND_SPLIT * both, EXTRA), bf16)
+    slots[me, :tok_count, piece:] = extra_ref[...]
+    for q in range(SEND_SPLIT):
+        cols = slice(q * piece, (q + 1) * piece)
+        slots[me, q * both : q * both + tok_count, :piece] = tokens_ref[:, cols]
+        slots[me, q * both + tok_count : (q + 1) * both, :piece] = cotangent_ref[:, cols]
     peers = [(None, core), (has_up, up), (has_down, down)]
     if n_y == 2:
         peers.append((None, side))
@@ -82,7 +89,6 @@
     def arrived(slot):
         copy(slot, core_sem, core).wait_recv()
 
-    own.wait()
     pl.when(has_up)(copy(me, up_sem, up).start)
     pl.when(has_down)(copy(me, down_sem, down).start)
     if n_y == 2:
@@ -100,6 +106,11 @@
 
         lax.fori_loop(0, width // step, lay, 0)
 
+    def clear(slot, carry):
+        wide[slot] = jnp.zeros((SLOT_ROWS, width), bf16)
+        return carry
+
+    lax.fori_loop(0, n, clear, 0)
     reach = jnp.minimum(z, n_z - 1 - z)
 
     def nearest(i):
@@ -130,9 +141,16 @@
             for lane in range(n_y):
                 arrived((1 - c) * n_inner + there * n_y + lane)
             places = [outer * n_inner + there * n_y for outer in range(n // n_inner)]
+            for place in places:
+                for slot in range(n_y):
+                    for q in range(SEND_SPLIT):
+                        cols = slice(q * piece, (q + 1) * piece)
+                        wide[place + slot, :both, cols] = slots[
+                            place + slot, q * both : (q + 1) * both, :piece
+                        ]
             rows = jnp.concatenate(
                 [
-                    slots[pl.ds(place, n_y), :, :width].reshape(n_y * SLOT_ROWS, width)
+                    wide[pl.ds(place, n_y)].reshape(n_y * SLOT_ROWS, width)
                     for place in places
                 ],
                 axis=0,
@@ -147,11 +165,11 @@
         return carry
 
     lax.fori_loop(0, n_z + 1, visit, 0)
-    save = pltpu.make_async_copy(slots, slots_out, out_sem)
+    save = pltpu.make_async_copy(wide, slots_out, out_sem)
     save.start()
 
     total = n * SLOT_ROWS
-    extra = slots[:, :, width:].reshape(total, slots.shape[2] - width).astype(f32)
+    extra = slots[:, :SLOT_ROWS, piece:].reshape(total, EXTRA).astype(f32)
     lane = lax.broadcasted_iota(jnp.int32, extra.shape, 1)
     column = lax.broadcasted_iota(jnp.int32, (total, joint), 1)
     weight = jnp.zeros((total, joint), f32)
@@ -171,7 +189,11 @@
     pre_up = grad_hidden * silu_gate
     for i, value in enumerate((pre_gate, pre_up, hidden)):
         left_ref[i] = value.T.astype(bf16)
-    compact = compact_ref[...]
+    place = lax.broadcasted_iota(jnp.int32, (n * tok_count, total), 1)
+    number = lax.broadcasted_iota(jnp.int32, (n * tok_count, total), 0)
+    within = place % SLOT_ROWS
+    compact = (place // SLOT_ROWS * tok_count + within == number) & (within < tok_count)
+    compact = jnp.where(compact, 1.0, 0.0).astype(bf16)
     few = [
         jnp.dot(compact, value.astype(bf16), preferred_element_type=f32).astype(bf16)
         for value in (pre_gate, pre_up)
@@ -198,32 +220,31 @@
     save.wait()
 
 
-def forward(rows, weights, n_outer, n_inner, tok_count):
+def forward(tokens, grad_out, extra, weights, n_outer, n_inner):
     n = n_outer * n_inner
+    tok_count = tokens.shape[0]
     hidden_count, local_count, width = weights[0].shape
     joint = hidden_count * local_count
     total = n * SLOT_ROWS
     bf16 = jnp.bfloat16
-    there = jnp.arange(n * tok_count, dtype=jnp.int32)
-    there = there // tok_count * SLOT_ROWS + there % tok_count
-    compact = (there[:, None] == jnp.arange(total, dtype=jnp.int32)[None, :]).astype(bf16)
     anywhere, vmem = pl.BlockSpec(memory_space=pl.ANY), pl.BlockSpec(memory_space=pltpu.VMEM)
-    slots = (n,) + rows.shape
+    slots = (n, SEND_SPLIT * 2 * tok_count, width // SEND_SPLIT + EXTRA)
+    wide = (n, SLOT_ROWS, width)
     return pl.pallas_call(
         functools.partial(forward_kernel, n_inner),
         out_shape=[
-            jax.ShapeDtypeStruct(slots, bf16),
+            jax.ShapeDtypeStruct(wide, bf16),
             jax.ShapeDtypeStruct((3, joint, total), bf16),
             jax.ShapeDtypeStruct((n * tok_count, width), bf16),
         ],
-        in_specs=[anywhere] * 4 + [vmem],
+        in_specs=[vmem] * 3 + [anywhere] * 3,
         out_specs=[anywhere, vmem, vmem],
         scratch_shapes=[
             pltpu.VMEM(slots, bf16),
+            pltpu.VMEM(wide, bf16),
             pltpu.VMEM((3,) + weights[0].shape, bf16),
             pltpu.VMEM((3, joint, width), bf16),
             pltpu.VMEM((3, n, SLOT_ROWS, joint), jnp.float32),
-            pltpu.SemaphoreType.DMA(()),
             pltpu.SemaphoreType.DMA((3,)),
             pltpu.SemaphoreType.DMA(()),
         ]
@@ -232,7 +253,7 @@
             collective_id=0, has_side_effects=True, vmem_limit_bytes=56 << 20
         ),
         name="forward",
-    )(rows, *weights, compact)
+    )(tokens, grad_out, extra, *weights)
 
 
 def back_kernel(
@@ -338,7 +359,7 @@
         + [pltpu.VMEM((n_z,) + block, bf16)] * 4
         + [pltpu.SemaphoreType.DMA((n_z,))] * 6,
         compiler_params=pltpu.CompilerParams(
-            collective_id=1, has_side_effects=True, vmem_limit_bytes=48 << 20
+            collective_id=1, has_side_effects=True, vmem_limit_bytes=(8 + n_inner) << 20
         ),
         name="sum_back",
     )(part)
@@ -369,11 +390,17 @@
     )(left, rows)
 
 
-def three_parts(value):
-    high = lax.reduce_precision(value, 8, 7)
-    middle = lax.reduce_precision(value - high, 8, 7)
-    low = value - high - middle
-    return [part.astype(jnp.bfloat16) for part in (high, middle, low)]
+def pair_columns(gate_probs, routes, n_flight):
+    lane = np.arange(EXTRA, dtype=np.int32)[None, :]
+    expert, which = lane % n_flight, lane // n_flight
+    weights = 0.0
+    for k in range(routes.shape[1]):
+        weights = weights + jnp.where(routes[:, k : k + 1] == expert, gate_probs[:, k : k + 1], 0.0)
+    high = lax.reduce_precision(weights, 8, 7)
+    middle = lax.reduce_precision(weights - high, 8, 7)
+    low = weights - high - middle
+    picked = jnp.where(which == 0, high, jnp.where(which == 1, middle, low))
+    return jnp.where(which < 3, picked, 0.0).astype(jnp.bfloat16)
 
 
 def local(tokens, grad_out, gate_probs, routes, w_gate, w_up, w_down):
@@ -383,22 +410,16 @@
     n = n_outer * n_inner
     n_flight = w_gate.shape[0] * n_outer
 
-    named = routes[:, :, None] == jnp.arange(n_flight, dtype=jnp.int32)[None, None, :]
-    weights = jnp.sum(jnp.where(named, gate_probs[:, :, None], 0.0), axis=1)
-    extra = jnp.concatenate(three_parts(weights), axis=1)
-    extra = jnp.pad(extra, ((0, SLOT_ROWS - tok_count), (0, EXTRA - extra.shape[1])))
-    rows = jnp.concatenate([tokens, grad_out], axis=0)
-    rows = jnp.pad(rows, ((0, SLOT_ROWS - 2 * tok_count), (0, 0)))
-    rows = jnp.concatenate([rows, extra], axis=1)
+    extra = pair_columns(gate_probs, routes, n_flight)
     turned = [jnp.transpose(w, (1, 0, 2)) for w in (w_gate, w_up, w_down)]
-    slots, left, part = forward(rows, turned, n_outer, n_inner, tok_count)
+    slots, left, part = forward(tokens, grad_out, extra, turned, n_outer, n_inner)
 
     part = part.reshape(n, tok_count, BACK_SPLIT, width // BACK_SPLIT)
     part = jnp.transpose(part, (0, 2, 1, 3)).reshape(n, BACK_SPLIT * tok_count, -1)
     back = sum_back(part, n_inner).reshape(BACK_SPLIT, tok_count, width // BACK_SPLIT)
     grad_tokens = jnp.transpose(back, (1, 0, 2)).reshape(tok_count, width)
 
-    flat = slots.reshape(n * SLOT_ROWS, width + EXTRA)
+    flat = slots.reshape(n * SLOT_ROWS, width)
     grads = weight_grads(left, flat, turned[0].shape)
     return (grad_tokens, *(jnp.transpose(grad, (1, 0, 2)) for grad in grads))
 

time: 72.4 us -> 67.4 us (0.931)
  Pallas kernels: 63.3 us -> 58.7 us
  other arithmetic: 3.27 us -> 1.36 us
  local copies, waits for them, and re-layouts: 4.91 us -> 6.31 us
    pallas_call x1, Pallas kernels: 42.5 us -> 37.6 us  [forward(): pl.pallas_call(functools.partial(forward_kernel, n_inner), out_shape=[jax...]
    concatenate x3 -> x0, other arithmetic: 1.83 us -> none  [the longest x1 1.05 us: local(): rows = jnp.concatenate([tokens, grad_out], axis=0)]
    broadcast_in_dim x0 -> x1, local copies, waits for them, and re-layouts: none -> 0.76 us  [pair_columns(): jnp.where(routes[:, k:k + 1] == expert, gate_probs[:, k:k + 1], 0.0)]
    eq x0 -> x1, local copies, waits for them, and re-layouts: none -> 0.76 us  [pair_columns(): routes[:, k:k + 1] == expert]
where the time goes in v4:
time: 67.4 us; the launch traced here: 67.1 us
  Pallas kernels  58.7 us (87%)
  local copies, waits for them, and re-layouts  6.31 us (9%)
  other arithmetic  1.36 us (2%)
  between operations  0.68 us (1%)
    pallas_call x1, Pallas kernels, forward(): pl.pallas_call(functools.partial(forward_kernel, n_inner), out_shape=[jax...  37.6 us
    pallas_call x1, Pallas kernels, sum_back(): pl.pallas_call(functools.partial(back_kernel, n_inner), out_shape=jax.Sha...  15.9 us
    pallas_call x1, Pallas kernels, weight_grads(): pl.pallas_call(grads_kernel, out_shape=[jax.ShapeDtypeStruct(shape, jnp.b...  5.25 us
    unnamed x5, local copies, waits for them, and re-layouts  3.61 us
    convert_element_type x1, other arithmetic, pair_columns(): return jnp.where(which < 3, picked, 0.0).astype(jnp.bfloat16)  1.36 us

profile of v4, /device:TPU:0, one launch (start us, length us, event | category | flops | bytes accessed | tf_op | source)
XLA Modules:
  0.0 67.1 jit_solution(10011819606797884495)
XLA Ops:
  0.6 0.8 %slice_bitcast_fusion.2 = (f32[6]{0:T(128)S(1)}, f32[6]{0:T(128)S(1)}) fusion(f32[6,2]{0,1:T(2,128)} %param.13), kind=kLoop, calls=%fused_computation.7 | loop fusion | bytes 96 | tf_op jit(solution)/shard_map/jit(_where)/broadcast_in_dim | solution.py:398
  1.4 0.8 %slice_bitcast_fusion.3 = (s32[6]{0:T(128)S(1)}, s32[6]{0:T(128)S(1)}) fusion(s32[6,2]{0,1:T(2,128)} %param.14), kind=kLoop, calls=%fused_computation.8 | loop fusion | bytes 96 | tf_op jit(solution)/shard_map/eq | solution.py:398
  2.1 1.4 %fusion.1.extra_ref = bf16[6,128]{1,0:T(8,128)(2,1)} fusion(f32[6]{0:T(128)S(1)} %get-tuple-element.19, f32[6]{0:T(128)S(1)} %get-tuple-element.18, s32[128]{0:T(128)} %constant.23, s32[6]{0:T(128)S(1)} %get-tuple-element.17, s32[6]{0:T(128)S(1)} %get-tuple-element.16, pred[128]{0:T(512)(128)(4,1)} %constant.24, pred[128]{0:T(512)(128)(4,1)} %constant.22, ...), kind=kLoop, calls=%fused_computation.4 | loop fusion | flops 9984 | bytes 2528 | tf_op jit(solution)/shard_map/convert_element_type | solution.py:403
  3.5 37.6 %forward.1 = (bf16[16,16,7168]{2,1,0:T(8,128)(2,1)}, bf16[3,152,256]{2,1,0:T(8,128)(2,1)}, bf16[96,7168]{1,0:T(8,128)(2,1)}) custom-call(bf16[6,7168]{1,0:T(8,128)(2,1)} %tokens_ref.1, bf16[6,7168]{1,0:T(8,128)(2,1)} %cotangent_ref.1, bf16[6,128]{1,0:T(8,128)(2,1)} %fusion.1.extra_ref, bf16[76,2,7168]{2,1,0:T(2,128)(2,1)} %bitcast.27, ...), custom_call_target="tpu_custom_call" | custom-call | tf_op jit(solution)/shard_map/forward/pallas_call | solution.py:233
  41.1 1.6 %copy.18 = bf16[12,8,8,896]{3,2,1,0:T(8,128)(2,1)S(1)} copy(bf16[12,8,8,896]{3,1,2,0:T(8,128)(2,1)} %bitcast.30) | data formatting | bytes 2752512
  42.7 0.3 copy.16
  43.0 0.0 copy-start.1
  43.0 0.3 copy.17.part_ref
  43.3 15.9 %sum_back.1 = bf16[48,896]{1,0:T(8,128)(2,1)S(1)} custom-call(bf16[16,48,896]{2,1,0:T(8,128)(2,1)S(1)} %copy.17.part_ref), custom_call_target="tpu_custom_call" | custom-call | tf_op jit(solution)/shard_map/sum_back/pallas_call | solution.py:350
  59.1 0.7 %reshape.25 = bf16[8,6,896]{2,1,0:T(8,128)(2,1)} reshape(bf16[48,896]{1,0:T(8,128)(2,1)S(1)} %sum_back.1) | data formatting | bytes 172032 | tf_op jit(solution)/shard_map/reshape | solution.py:419
  59.8 0.0 copy-done.1
  59.8 0.0 copy-start
  59.8 2.0 %copy-done = bf16[16,16,7168]{2,1,0:T(8,128)(2,1)S(1)} copy-done((bf16[16,16,7168]{2,1,0:T(8,128)(2,1)S(1)}, bf16[16,16,7168]{2,1,0:T(8,128)(2,1)}, u32[]{:S(2)}) %copy-start) | copy-done | bytes 3670040
  61.8 5.3 %weight_grads.1 = (bf16[76,2,7168]{2,1,0:T(2,128)(2,1)}, bf16[76,2,7168]{2,1,0:T(2,128)(2,1)}, bf16[76,2,7168]{2,1,0:T(2,128)(2,1)}) custom-call(bf16[3,152,256]{2,1,0:T(8,128)(2,1)S(1)} %copy-done.1, bf16[256,7168]{1,0:T(8,128)(2,1)S(1)} %bitcast.24), custom_call_target="tpu_custom_call" | custom-call | tf_op jit(solution)/shard_map/weight_grads/pallas_call | solution.py:379
Async XLA Ops:
  43.0 16.8 %copy-start.1 = (bf16[3,152,256]{2,1,0:T(8,128)(2,1)S(1)}, bf16[3,152,256]{2,1,0:T(8,128)(2,1)}, u32[]{:S(2)}) copy-start(bf16[3,152,256]{2,1,0:T(8,128)(2,1)} %get-tuple-element.11.left_ref) | copy-start | bytes 700420
  59.8 2.0 %copy-start = (bf16[16,16,7168]{2,1,0:T(8,128)(2,1)S(1)}, bf16[16,16,7168]{2,1,0:T(8,128)(2,1)}, u32[]{:S(2)}) copy-start(bf16[16,16,7168]{2,1,0:T(8,128)(2,1)} %get-tuple-element.12) | copy-start | bytes 11010052

commit v5 on v4

--- a/solution.py
+++ b/solution.py
@@ -1,7 +1,6 @@
 import functools
 import jax
 import jax.numpy as jnp
-import numpy as np
 from jax import lax
 from jax.experimental import pallas as pl
 from jax.experimental.pallas import tpu as pltpu
@@ -36,8 +35,31 @@
     pl.semaphore_wait(barrier, count)
 
 
+def pair_columns(probs_ref, routes_ref, n_flight):
+    f32, bf16 = jnp.float32, jnp.bfloat16
+    top_k, tok_count = probs_ref.shape
+    square = (tok_count, tok_count)
+    same = lax.broadcasted_iota(jnp.int32, square, 0) == lax.broadcasted_iota(jnp.int32, square, 1)
+
+    def upright(row):
+        return jnp.sum(jnp.where(same, jnp.broadcast_to(row, square), 0.0), axis=1, keepdims=True)
+
+    lane = lax.broadcasted_iota(jnp.int32, (tok_count, EXTRA), 1)
+    expert, which = (lane % n_flight).astype(f32), lane // n_flight
+    weights = jnp.zeros((tok_count, EXTRA), f32)
+    for k in range(top_k):
+        prob = upright(probs_ref[k : k + 1, :])
+        route = upright(routes_ref[k : k + 1, :].astype(f32))
+        weights = weights + jnp.where(route == expert, prob, 0.0)
+    high = weights.astype(bf16).astype(f32)
+    middle = (weights - high).astype(bf16).astype(f32)
+    low = weights - high - middle
+    picked = jnp.where(which == 0, high, jnp.where(which == 1, middle, low))
+    return jnp.where(which < 3, picked, 0.0).astype(bf16)
+
+
 def forward_kernel(
-    n_inner, tokens_ref, cotangent_ref, extra_ref, gate_hbm, up_hbm, down_hbm,
+    n_inner, tokens_ref, cotangent_ref, probs_ref, routes_ref, gate_hbm, up_hbm, down_hbm,
     slots_out, left_ref, part_ref, slots, wide, raw, flat_w, products, raw_sem, out_sem, up_sem, down_sem, side_sem, core_sem, recv_sem,
 ):
     n_y = lanes_of(n_inner)
@@ -66,7 +88,7 @@
     for load in loads:
         load.start()
     slots[me, :, piece:] = jnp.zeros((SEND_SPLIT * both, EXTRA), bf16)
-    slots[me, :tok_count, piece:] = extra_ref[...]
+    slots[me, :tok_count, piece:] = pair_columns(probs_ref, routes_ref, n_flight)
     for q in range(SEND_SPLIT):
         cols = slice(q * piece, (q + 1) * piece)
         slots[me, q * both : q * both + tok_count, :piece] = tokens_ref[:, cols]
@@ -220,7 +242,7 @@
     save.wait()
 
 
-def forward(tokens, grad_out, extra, weights, n_outer, n_inner):
+def forward(tokens, grad_out, gate_probs, routes, weights, n_outer, n_inner):
     n = n_outer * n_inner
     tok_count = tokens.shape[0]
     hidden_count, local_count, width = weights[0].shape
@@ -237,7 +259,7 @@
             jax.ShapeDtypeStruct((3, joint, total), bf16),
             jax.ShapeDtypeStruct((n * tok_count, width), bf16),
         ],
-        in_specs=[vmem] * 3 + [anywhere] * 3,
+        in_specs=[vmem] * 4 + [anywhere] * 3,
         out_specs=[anywhere, vmem, vmem],
         scratch_shapes=[
             pltpu.VMEM(slots, bf16),
@@ -253,7 +275,7 @@
             collective_id=0, has_side_effects=True, vmem_limit_bytes=56 << 20
         ),
         name="forward",
-    )(tokens, grad_out, extra, *weights)
+    )(tokens, grad_out, gate_probs.T, routes.T, *weights)
 
 
 def back_kernel(
@@ -385,22 +407,9 @@
             pl.BlockSpec((rows.shape[0], step), lambda i: (0, i)),
         ],
         out_specs=[out] * 3,
-        compiler_params=pltpu.CompilerParams(vmem_limit_bytes=40 << 20),
+        compiler_params=pltpu.CompilerParams(vmem_limit_bytes=60 << 20),
         name="weight_grads",
     )(left, rows)
-
-
-def pair_columns(gate_probs, routes, n_flight):
-    lane = np.arange(EXTRA, dtype=np.int32)[None, :]
-    expert, which = lane % n_flight, lane // n_flight
-    weights = 0.0
-    for k in range(routes.shape[1]):
-        weights = weights + jnp.where(routes[:, k : k + 1] == expert, gate_probs[:, k : k + 1], 0.0)
-    high = lax.reduce_precision(weights, 8, 7)
-    middle = lax.reduce_precision(weights - high, 8, 7)
-    low = weights - high - middle
-    picked = jnp.where(which == 0, high, jnp.where(which == 1, middle, low))
-    return jnp.where(which < 3, picked, 0.0).astype(jnp.bfloat16)
 
 
 def local(tokens, grad_out, gate_probs, routes, w_gate, w_up, w_down):
@@ -408,11 +417,11 @@
     n_outer = lax.axis_size("inter")
     n_inner = lax.axis_size("intra")
     n = n_outer * n_inner
-    n_flight = w_gate.shape[0] * n_outer
-
-    extra = pair_columns(gate_probs, routes, n_flight)
+
     turned = [jnp.transpose(w, (1, 0, 2)) for w in (w_gate, w_up, w_down)]
-    slots, left, part = forward(tokens, grad_out, extra, turned, n_outer, n_inner)
+    slots, left, part = forward(
+        tokens, grad_out, gate_probs, routes, turned, n_outer, n_inner
+    )
 
     part = part.reshape(n, tok_count, BACK_SPLIT, width // BACK_SPLIT)
     part = jnp.transpose(part, (0, 2, 1, 3)).reshape(n, BACK_SPLIT * tok_count, -1)

time: 67.4 us -> 64.6 us (0.958)
  local copies, waits for them, and re-layouts: 6.31 us -> 2.75 us
  Pallas kernels: 58.7 us -> 60.9 us
  other arithmetic: 1.36 us -> 0 us
    pallas_call x1, Pallas kernels: 5.25 us -> 7.34 us  [weight_grads(): pl.pallas_call(grads_kernel, out_shape=[jax.ShapeDtypeStruct(shape, jnp.b...]
    unnamed x5 -> x1, local copies, waits for them, and re-layouts: 3.61 us -> 1.57 us
    convert_element_type x1 -> x0, other arithmetic: 1.36 us -> none  [pair_columns(): return jnp.where(which < 3, picked, 0.0).astype(jnp.bfloat16)]
    broadcast_in_dim x1 -> x0, local copies, waits for them, and re-layouts: 0.76 us -> none  [pair_columns(): jnp.where(routes[:, k:k + 1] == expert, gate_probs[:, k:k + 1], 0.0)]
    eq x1 -> x0, local copies, waits for them, and re-layouts: 0.76 us -> none  [pair_columns(): routes[:, k:k + 1] == expert]
where the time goes in v5:
time: 64.6 us; the launch traced here: 64.3 us
  Pallas kernels  60.9 us (94%)
  local copies, waits for them, and re-layouts  2.75 us (4%)
  between operations  0.67 us (1%)
    pallas_call x1, Pallas kernels, forward(): pl.pallas_call(functools.partial(forward_kernel, n_inner), out_shape=[jax...  37.7 us
    pallas_call x1, Pallas kernels, sum_back(): pl.pallas_call(functools.partial(back_kernel, n_inner), out_shape=jax.Sha...  15.9 us
    pallas_call x1, Pallas kernels, weight_grads(): pl.pallas_call(grads_kernel, out_shape=[jax.ShapeDtypeStruct(shape, jnp.b...  7.34 us
    unnamed x1, local copies, waits for them, and re-layouts  1.57 us

profile of v5, /device:TPU:0, one launch (start us, length us, event | category | flops | bytes accessed | tf_op | source)
XLA Modules:
  0.0 64.3 jit_solution(16601454434153978889)
XLA Ops:
  0.6 37.7 %forward.1 = (bf16[16,16,7168]{2,1,0:T(8,128)(2,1)}, bf16[3,152,256]{2,1,0:T(8,128)(2,1)}, bf16[96,7168]{1,0:T(8,128)(2,1)}) custom-call(bf16[6,7168]{1,0:T(8,128)(2,1)} %tokens_ref.1, bf16[6,7168]{1,0:T(8,128)(2,1)} %cotangent_ref.1, f32[2,6]{1,0:T(2,128)} %bitcast.26, s32[2,6]{1,0:T(2,128)} %bitcast.27, bf16[76,2,7168]{2,1,0:T(2,128)(2,1)} %bitcast.21, ...), custom_call_target="tpu_custom_call" | custom-call | tf_op jit(solution)/shard_map/forward/pallas_call | solution.py:255
  38.3 1.6 %copy.14 = bf16[12,8,8,896]{3,2,1,0:T(8,128)(2,1)S(1)} copy(bf16[12,8,8,896]{3,1,2,0:T(8,128)(2,1)} %bitcast.24) | data formatting | bytes 2752512
  39.9 0.3 copy.12
  40.1 0.3 copy.13.part_ref
  40.4 15.9 %sum_back.1 = bf16[48,896]{1,0:T(8,128)(2,1)S(1)} custom-call(bf16[16,48,896]{2,1,0:T(8,128)(2,1)S(1)} %copy.13.part_ref), custom_call_target="tpu_custom_call" | custom-call | tf_op jit(solution)/shard_map/sum_back/pallas_call | solution.py:372
  56.3 0.7 %reshape.25 = bf16[8,6,896]{2,1,0:T(8,128)(2,1)} reshape(bf16[48,896]{1,0:T(8,128)(2,1)S(1)} %sum_back.1) | data formatting | bytes 172032 | tf_op jit(solution)/shard_map/reshape | solution.py:428
  57.0 7.3 %weight_grads.1 = (bf16[76,2,7168]{2,1,0:T(2,128)(2,1)}, bf16[76,2,7168]{2,1,0:T(2,128)(2,1)}, bf16[76,2,7168]{2,1,0:T(2,128)(2,1)}) custom-call(bf16[3,152,256]{2,1,0:T(8,128)(2,1)} %get-tuple-element.11.left_ref, bf16[256,7168]{1,0:T(8,128)(2,1)} %bitcast.20), custom_call_target="tpu_custom_call" | custom-call | tf_op jit(solution)/shard_map/weight_grads/pallas_call | solution.py:401
